TPU v7x, 32 devices: a whole 2x2x4 slice. The times are simulated.
32 devices in a mesh: groups: 2 (over y), gx: 4 (over z), gy: 4 (over x, core).
Axes of the slice: x: 2, y: 2, z: 4, core: 2. Of those that a mesh axis runs over, the one named last changes fastest.
Arguments:
- courant: float32 [32, 256, 128], P('gx', 'gy'), may hold values from 0.04 to 0.16
- state_prev: float32 [64, 256, 128], P(('groups', 'gx'), 'gy'), parts along dimension 0, may hold values from -6 to 6
- state_now: float32 [64, 256, 128], P(('groups', 'gx'), 'gy'), parts along dimension 0, may hold values from -6 to 6
- adjoint_now: float32 [64, 256, 128], P(('groups', 'gx'), 'gy'), parts along dimension 0, may hold values from -6 to 6
- adjoint_next: float32 [64, 256, 128], P(('groups', 'gx'), 'gy'), parts along dimension 0, may hold values from -6 to 6
- source_cell: int32 [32], P('groups'), parts along dimension 0, may hold values from 0 to 1048575
- wavelet: float32 [12, 32], P(None, 'groups'), parts along dimension 1, may hold values from -24 to 24
- observed: float32 [24, 4, 4, 4, 128], P('groups', 'gx', 'gy'), parts along dimension 0, may hold values from -6 to 6
- receiver_cell: int32 [4, 4, 4, 128], P('gx', 'gy'), may hold values from 0 to 65535
- receiver_count: int32 [4, 4, 4], P('gx', 'gy'), may hold values from 0 to 128, as said below
Outputs:
- gradient: float32 [64, 256, 128], P(('groups', 'gx'), 'gy'), parts along dimension 0
- trace_residual: float32 [24, 4, 4, 4, 128], P('groups', 'gx', 'gy'), parts along dimension 0
There are 2 independent parts, one for each index of `groups`. A program takes and returns all parts, laid end to end along the dimension named above; an argument that names none is the same for every part. Nothing has to cross between parts.
Inputs may be any that keep to these rules, and one draw needn't show every extreme that they name: receiver_count[k, j, i] counts the used slots that trace tile (i, j) holds for slab k; in every draw one slab k takes 128 from every tile i of strip 0.
All inputs are finite; a program needn't handle non-finite values.
Results may differ from a plain program's by a relative error of at most 0.00002.
Values sent between devices are 32-bit elements; how exact they have to be, the bound alone decides.
No kernel may reach another device: no remote copies, remote signals or barrier semaphores. Data moves between devices by JAX's collectives and lax.ppermute only.
A program may use at most 64 MiB of HBM per device.

v0:
```python
import jax
import jax.numpy as jnp
from jax import lax
from jax.sharding import PartitionSpec as P

STEPS = 12
SPONGE = 8


stencil = (-205.0 / 72.0, 8.0 / 5.0, -1.0 / 5.0, 8.0 / 315.0, -1.0 / 560.0)
damping_peak = 0.3


def padded_2(cells, sides, width):
    for axis, dim in sides:
        count = lax.axis_size(axis)
        ends = count - 1
        head = lax.slice_in_dim(cells, 0, width, axis=dim)
        tail = lax.slice_in_dim(cells, cells.shape[dim] - width, cells.shape[dim], axis=dim)
        cells = jnp.concatenate(
            [
                lax.ppermute(tail, axis, [(i, (i + 1) % count) for i in range(ends)]),
                cells,
                lax.ppermute(head, axis, [((i + 1) % count, i) for i in range(ends)]),
            ],
            axis=dim,
        )
    return cells


def laplace(values):
    width_x, width_y, depth_z = values.shape
    padded = padded_2(values, (("gx", 0), ("gy", 1)), 4)
    z_padded = jnp.pad(values, ((0, 0), (0, 0), (4, 4)))
    summed = 3.0 * stencil[0] * values
    for offset in range(1, 5):
        paired = (
            padded[4 + offset : 4 + offset + width_x, 4 : 4 + width_y]
            + padded[4 - offset : 4 - offset + width_x, 4 : 4 + width_y]
        )
        paired = (
            paired
            + padded[4 : 4 + width_x, 4 + offset : 4 + offset + width_y]
            + padded[4 : 4 + width_x, 4 - offset : 4 - offset + width_y]
        )
        paired = (
            paired
            + z_padded[:, :, 4 + offset : 4 + offset + depth_z]
            + z_padded[:, :, 4 - offset : 4 - offset + depth_z]
        )
        summed = summed + stencil[offset] * paired
    return summed


def sponge(start, count, whole):
    position = start + jnp.arange(count, dtype=jnp.int32)
    edge_gap = jnp.minimum(position, whole - 1 - position)
    profile = jnp.maximum(SPONGE - edge_gap, 0).astype(jnp.float32) / SPONGE
    return profile * profile


def place_sum(indices, amounts, shape):
    flat = jnp.zeros((shape[0] * shape[1] * shape[2],), jnp.float32).at[indices].add(amounts)
    return flat.reshape(shape)


def local(
    courant,
    state_prev,
    state_now,
    adjoint_now,
    adjoint_next,
    source_cell,
    wavelet,
    observed,
    receiver_cell,
    receiver_count,
):
    shape = courant.shape
    width_x, width_y, depth_z = shape
    slab = lax.axis_index("gx")
    strip = lax.axis_index("gy")
    whole_x = width_x * lax.axis_size("gx")
    whole_y = width_y * lax.axis_size("gy")
    damping = damping_peak * (
        sponge(slab * width_x, width_x, whole_x)[:, None, None]
        + sponge(strip * width_y, width_y, whole_y)[None, :, None]
    )
    source_x = source_cell // (whole_y * depth_z) - slab * width_x
    source_y = source_cell // depth_z % whole_y - strip * width_y
    source_z = source_cell % depth_z
    inside = (source_x >= 0) & (source_x < width_x) & (source_y >= 0) & (source_y < width_y)
    source_flat = jnp.where(inside, (source_x * width_y + source_y) * depth_z + source_z, 0)
    source_weight = wavelet * inside.astype(jnp.float32)[None, :]
    senders = receiver_cell.shape[2]
    slots = receiver_cell.shape[3]
    cells = receiver_cell.reshape(-1)
    active = (
        jnp.arange(slots, dtype=jnp.int32)[None, :] < receiver_count.reshape(senders, 1)
    ).astype(jnp.float32)
    active_flat = active.reshape(-1)

    def advance(carry, weights):
        former, current = carry
        drive = laplace(current) + place_sum(source_flat, weights, shape)
        following = (2.0 * current - (1.0 - damping) * former + courant * drive) / (1.0 + damping)
        return (
            (current, following),
            (following - 2.0 * current + former, following.reshape(-1)[cells] * active_flat),
        )

    final_states, (accels, recorded) = lax.scan(advance, (state_prev, state_now), source_weight)
    recorded_tiles = recorded.reshape(STEPS, senders, 1, 1, slots)
    active_tiles = active.reshape(1, senders, 1, 1, slots)
    synthetic, mask_back = (
        lax.all_to_all(recorded_tiles, "gx", split_axis=1, concat_axis=3, tiled=True),
        lax.all_to_all(active_tiles, "gx", split_axis=1, concat_axis=3, tiled=True),
    )
    trace_residual = mask_back * (synthetic - observed)
    misfit = lax.all_to_all(trace_residual, "gx", split_axis=3, concat_axis=1, tiled=True)
    misfit_rows = misfit.reshape(STEPS, senders * slots)

    def retreat(carry, inputs):
        later, current, gradient = carry
        acceleration, residual_row = inputs
        drive = laplace(current) + place_sum(cells, residual_row, shape)
        earlier = (2.0 * current - (1.0 - damping) * later + courant * drive) / (1.0 + damping)
        return ((current, earlier, gradient + earlier * acceleration), None)

    start_gradient = jnp.zeros(shape, jnp.float32)
    (last_later, last_current, gradient), unused = lax.scan(
        retreat, (adjoint_next, adjoint_now, start_gradient), (accels, misfit_rows), reverse=True
    )
    return (gradient, trace_residual)


def solution(mesh):
    placed = (
        P("gx", "gy", None),
        P(("groups", "gx"), "gy", None),
        P(("groups", "gx"), "gy", None),
        P(("groups", "gx"), "gy", None),
        P(("groups", "gx"), "gy", None),
        P("groups"),
        P(None, "groups"),
        P("groups", "gx", "gy", None, None),
        P("gx", "gy", None, None),
        P("gx", "gy", None),
    )
    return jax.shard_map(
        local,
        mesh=mesh,
        in_specs=placed,
        out_specs=(P(("groups", "gx"), "gy", None), P("groups", "gx", "gy", None, None)),
        check_vma=False,
    )
```

profile of v0, /device:TPU:0, one launch (start us, length us, event | category | flops | bytes accessed | tf_op | source)
XLA Modules:
  0.0 532.2 jit_solution(455857605726409822)
XLA Ops:
  3.8 6.3 %all-to-all-start = ((f32[1,4,1,1,128]{4,3,2,0,1:T(1,128)}), f32[1,4,1,1,128]{4,3,2,0,1:T(1,128)S(1)}, u32[]{:S(2)}, u32[]{:S(2)}) async-start(f32[1,4,1,1,128]{4,3,2,0,1:T(1,128)} %compare_convert_fusion), calls=%async_computation | async-start | bytes 4096 | tf_op jit(solution)/shard_map/all_to_all | solution.py:117
  12.2 265.4 %while.38 = (s32[]{:T(128)}, f32[8,64,128]{2,1,0:T(8,128)S(1)}, f32[8,64,128]{2,1,0:T(8,128)S(1)}, f32[12,8,64,128]{3,2,1,0:T(8,128)}, f32[12,512]{1,0:T(8,128)S...) while((s32[]{:T(128)}, f32[8,64,128]{2,1,0:T(8,128)S(1)}, ...), condition=%wide.region_2.3_spmd.clone, body=%wide.region_0.2_spmd.clone.sunk | while | flops 3020866 | bytes 9405393 | solution.py:112
  19.0 4.3 collective-permute-done.1
  41.2 4.3 collective-permute-done.1
  64.4 4.3 collective-permute-done.1
  86.2 4.3 collective-permute-done.1
  108.0 4.3 collective-permute-done.1
  129.7 4.3 collective-permute-done.1
  151.5 4.3 collective-permute-done.1
  173.3 4.3 collective-permute-done.1
  195.1 4.3 collective-permute-done.1
  216.8 4.3 collective-permute-done.1
  238.6 4.3 collective-permute-done.1
  260.4 4.3 collective-permute-done.1
  277.7 8.0 %all_to_all.30 = f32[12,4,1,1,128]{4,3,2,0,1:T(1,128)S(1)} all-to-all(f32[12,4,1,1,128]{4,3,2,0,1:T(1,128)S(1)} %copy.25), channel_id=1, replica_groups=mesh['groups'=2,'gx'=4,'gy'=4] {'gx'}, dimensions={1} | all-to-all | bytes 49152 | tf_op jit(solution)/shard_map/all_to_all | solution.py:116
  289.6 5.6 %all-to-all-done.2 = f32[12,1,1,4,128]{4,0,2,1,3:T(8,128)S(1)} async-done(((f32[12,1,1,4,128]{4,0,2,1,3:T(8,128)}), f32[12,1,1,4,128]{4,0,2,1,3:T(8,128)S(1)}, u32[]{:S(2)}, u32[]{:S(2)}) %all-to-all-start.2) | async-done | bytes 24608 | tf_op jit(solution)/shard_map/all_to_all | solution.py:120
  295.3 236.2 %while.39 = (s32[]{:T(128)}, f32[8,64,128]{2,1,0:T(8,128)S(1)}, f32[8,64,128]{2,1,0:T(8,128)S(1)}, f32[8,64,128]{2,1,0:T(8,128)S(1)}, s32[512]{0:T(512)}, /*inde...) while((s32[]{:T(128)}, f32[8,64,128]{2,1,0:T(8,128)S(1)}, ...), condition=%wide.region_5.6_spmd.clone, body=%wide.region_3.5_spmd.clone.sunk | while | flops 3084292 | bytes 9912935 | solution.py:131
  318.9 4.3 collective-permute-done.5
  339.1 4.3 collective-permute-done.5
  358.8 4.3 collective-permute-done.5
  378.5 4.3 collective-permute-done.5
  398.2 4.3 collective-permute-done.5
  417.9 4.3 collective-permute-done.5
  457.3 4.3 collective-permute-done.5
  (575 shorter events, 427.3 us)
Async XLA Ops:
  3.8 273.8 %all-to-all-start = ((f32[1,4,1,1,128]{4,3,2,0,1:T(1,128)}), f32[1,4,1,1,128]{4,3,2,0,1:T(1,128)S(1)}, u32[]{:S(2)}, u32[]{:S(2)}) async-start(f32[1,4,1,1,128]{4,3,2,0,1:T(1,128)} %compare_convert_fusion), calls=%async_computation | async-start | bytes 4096 | tf_op jit(solution)/shard_map/all_to_all | solution.py:117
  16.4 6.9 %collective-permute-start.1 = (f32[4,64,128]{2,1,0:T(8,128)S(1)}, f32[4,64,128]{2,1,0:T(8,128)S(1)}, u32[]{:S(2)}, u32[]{:S(2)}) collective-permute-start(f32[4,64,128]{2,1,0:T(8,128)S(1)} %get-tuple-element.634), channel_id=1, source_target_pairs={{4,0},{8,4},{12,8},{5,1},{9,5},{13,9},{6,2},{10,6},{14,10},{7,3},{... | collective-permute-start | bytes 393224 | tf_op jit(solution)/shard_map/while/body/eval_jaxpr/ppermute | solution.py:24
  38.6 6.9 %collective-permute-start.1 = (f32[4,64,128]{2,1,0:T(8,128)S(1)}, f32[4,64,128]{2,1,0:T(8,128)S(1)}, u32[]{:S(2)}, u32[]{:S(2)}) collective-permute-start(f32[4,64,128]{2,1,0:T(8,128)S(1)} %get-tuple-element.634), channel_id=1, source_target_pairs={{4,0},{8,4},{12,8},{5,1},{9,5},{13,9},{6,2},{10,6},{14,10},{7,3},{... | collective-permute-start | bytes 393224 | tf_op jit(solution)/shard_map/while/body/eval_jaxpr/ppermute | solution.py:24
  61.8 6.9 %collective-permute-start.1 = (f32[4,64,128]{2,1,0:T(8,128)S(1)}, f32[4,64,128]{2,1,0:T(8,128)S(1)}, u32[]{:S(2)}, u32[]{:S(2)}) collective-permute-start(f32[4,64,128]{2,1,0:T(8,128)S(1)} %get-tuple-element.634), channel_id=1, source_target_pairs={{4,0},{8,4},{12,8},{5,1},{9,5},{13,9},{6,2},{10,6},{14,10},{7,3},{... | collective-permute-start | bytes 393224 | tf_op jit(solution)/shard_map/while/body/eval_jaxpr/ppermute | solution.py:24
  83.6 6.9 %collective-permute-start.1 = (f32[4,64,128]{2,1,0:T(8,128)S(1)}, f32[4,64,128]{2,1,0:T(8,128)S(1)}, u32[]{:S(2)}, u32[]{:S(2)}) collective-permute-start(f32[4,64,128]{2,1,0:T(8,128)S(1)} %get-tuple-element.634), channel_id=1, source_target_pairs={{4,0},{8,4},{12,8},{5,1},{9,5},{13,9},{6,2},{10,6},{14,10},{7,3},{... | collective-permute-start | bytes 393224 | tf_op jit(solution)/shard_map/while/body/eval_jaxpr/ppermute | solution.py:24
  105.4 6.9 %collective-permute-start.1 = (f32[4,64,128]{2,1,0:T(8,128)S(1)}, f32[4,64,128]{2,1,0:T(8,128)S(1)}, u32[]{:S(2)}, u32[]{:S(2)}) collective-permute-start(f32[4,64,128]{2,1,0:T(8,128)S(1)} %get-tuple-element.634), channel_id=1, source_target_pairs={{4,0},{8,4},{12,8},{5,1},{9,5},{13,9},{6,2},{10,6},{14,10},{7,3},{... | collective-permute-start | bytes 393224 | tf_op jit(solution)/shard_map/while/body/eval_jaxpr/ppermute | solution.py:24
  127.1 6.9 %collective-permute-start.1 = (f32[4,64,128]{2,1,0:T(8,128)S(1)}, f32[4,64,128]{2,1,0:T(8,128)S(1)}, u32[]{:S(2)}, u32[]{:S(2)}) collective-permute-start(f32[4,64,128]{2,1,0:T(8,128)S(1)} %get-tuple-element.634), channel_id=1, source_target_pairs={{4,0},{8,4},{12,8},{5,1},{9,5},{13,9},{6,2},{10,6},{14,10},{7,3},{... | collective-permute-start | bytes 393224 | tf_op jit(solution)/shard_map/while/body/eval_jaxpr/ppermute | solution.py:24
  148.9 6.9 %collective-permute-start.1 = (f32[4,64,128]{2,1,0:T(8,128)S(1)}, f32[4,64,128]{2,1,0:T(8,128)S(1)}, u32[]{:S(2)}, u32[]{:S(2)}) collective-permute-start(f32[4,64,128]{2,1,0:T(8,128)S(1)} %get-tuple-element.634), channel_id=1, source_target_pairs={{4,0},{8,4},{12,8},{5,1},{9,5},{13,9},{6,2},{10,6},{14,10},{7,3},{... | collective-permute-start | bytes 393224 | tf_op jit(solution)/shard_map/while/body/eval_jaxpr/ppermute | solution.py:24
  170.7 6.9 %collective-permute-start.1 = (f32[4,64,128]{2,1,0:T(8,128)S(1)}, f32[4,64,128]{2,1,0:T(8,128)S(1)}, u32[]{:S(2)}, u32[]{:S(2)}) collective-permute-start(f32[4,64,128]{2,1,0:T(8,128)S(1)} %get-tuple-element.634), channel_id=1, source_target_pairs={{4,0},{8,4},{12,8},{5,1},{9,5},{13,9},{6,2},{10,6},{14,10},{7,3},{... | collective-permute-start | bytes 393224 | tf_op jit(solution)/shard_map/while/body/eval_jaxpr/ppermute | solution.py:24
  192.5 6.9 %collective-permute-start.1 = (f32[4,64,128]{2,1,0:T(8,128)S(1)}, f32[4,64,128]{2,1,0:T(8,128)S(1)}, u32[]{:S(2)}, u32[]{:S(2)}) collective-permute-start(f32[4,64,128]{2,1,0:T(8,128)S(1)} %get-tuple-element.634), channel_id=1, source_target_pairs={{4,0},{8,4},{12,8},{5,1},{9,5},{13,9},{6,2},{10,6},{14,10},{7,3},{... | collective-permute-start | bytes 393224 | tf_op jit(solution)/shard_map/while/body/eval_jaxpr/ppermute | solution.py:24
  214.2 6.9 %collective-permute-start.1 = (f32[4,64,128]{2,1,0:T(8,128)S(1)}, f32[4,64,128]{2,1,0:T(8,128)S(1)}, u32[]{:S(2)}, u32[]{:S(2)}) collective-permute-start(f32[4,64,128]{2,1,0:T(8,128)S(1)} %get-tuple-element.634), channel_id=1, source_target_pairs={{4,0},{8,4},{12,8},{5,1},{9,5},{13,9},{6,2},{10,6},{14,10},{7,3},{... | collective-permute-start | bytes 393224 | tf_op jit(solution)/shard_map/while/body/eval_jaxpr/ppermute | solution.py:24
  286.3 8.9 %all-to-all-start.2 = ((f32[12,1,1,4,128]{4,0,2,1,3:T(8,128)}), f32[12,1,1,4,128]{4,0,2,1,3:T(8,128)S(1)}, u32[]{:S(2)}, u32[]{:S(2)}) async-start(f32[12,1,1,4,128]{4,0,2,1,3:T(8,128)} %copy.28), calls=%async_computation.2 | async-start | bytes 65536 | tf_op jit(solution)/shard_map/all_to_all | solution.py:120
  298.0 7.3 %collective-permute-start.5 = (f32[4,64,128]{2,1,0:T(8,128)S(1)}, f32[4,64,128]{2,1,0:T(8,128)S(1)}, u32[]{:S(2)}, u32[]{:S(2)}) collective-permute-start(f32[4,64,128]{2,1,0:T(8,128)S(1)} %get-tuple-element.659), channel_id=1, source_target_pairs={{4,0},{8,4},{12,8},{5,1},{9,5},{13,9},{6,2},{10,6},{14,10},{7,3},{... | collective-permute-start | bytes 393224 | tf_op jit(solution)/shard_map/while/body/eval_jaxpr/ppermute | solution.py:24
  323.2 7.9 %collective-permute-start.6 = (f32[16,4,128]{2,1,0:T(4,128)S(1)}, f32[16,4,128]{2,1,0:T(4,128)S(1)}, u32[]{:S(2)}, u32[]{:S(2)}) collective-permute-start(f32[16,4,128]{2,1,0:T(4,128)S(1)} %get-tuple-element.662), channel_id=1, source_target_pairs={{0,1},{1,2},{2,3},{4,5},{5,6},{6,7},{8,9},{9,10},{10,11},{12,13},{... | collective-permute-start | bytes 98312 | tf_op jit(solution)/shard_map/while/body/eval_jaxpr/ppermute | solution.py:22
  343.5 7.9 %collective-permute-start.6 = (f32[16,4,128]{2,1,0:T(4,128)S(1)}, f32[16,4,128]{2,1,0:T(4,128)S(1)}, u32[]{:S(2)}, u32[]{:S(2)}) collective-permute-start(f32[16,4,128]{2,1,0:T(4,128)S(1)} %get-tuple-element.662), channel_id=1, source_target_pairs={{0,1},{1,2},{2,3},{4,5},{5,6},{6,7},{8,9},{9,10},{10,11},{12,13},{... | collective-permute-start | bytes 98312 | tf_op jit(solution)/shard_map/while/body/eval_jaxpr/ppermute | solution.py:22
  363.1 7.9 %collective-permute-start.6 = (f32[16,4,128]{2,1,0:T(4,128)S(1)}, f32[16,4,128]{2,1,0:T(4,128)S(1)}, u32[]{:S(2)}, u32[]{:S(2)}) collective-permute-start(f32[16,4,128]{2,1,0:T(4,128)S(1)} %get-tuple-element.662), channel_id=1, source_target_pairs={{0,1},{1,2},{2,3},{4,5},{5,6},{6,7},{8,9},{9,10},{10,11},{12,13},{... | collective-permute-start | bytes 98312 | tf_op jit(solution)/shard_map/while/body/eval_jaxpr/ppermute | solution.py:22
  382.8 7.9 %collective-permute-start.6 = (f32[16,4,128]{2,1,0:T(4,128)S(1)}, f32[16,4,128]{2,1,0:T(4,128)S(1)}, u32[]{:S(2)}, u32[]{:S(2)}) collective-permute-start(f32[16,4,128]{2,1,0:T(4,128)S(1)} %get-tuple-element.662), channel_id=1, source_target_pairs={{0,1},{1,2},{2,3},{4,5},{5,6},{6,7},{8,9},{9,10},{10,11},{12,13},{... | collective-permute-start | bytes 98312 | tf_op jit(solution)/shard_map/while/body/eval_jaxpr/ppermute | solution.py:22
  402.5 7.9 %collective-permute-start.6 = (f32[16,4,128]{2,1,0:T(4,128)S(1)}, f32[16,4,128]{2,1,0:T(4,128)S(1)}, u32[]{:S(2)}, u32[]{:S(2)}) collective-permute-start(f32[16,4,128]{2,1,0:T(4,128)S(1)} %get-tuple-element.662), channel_id=1, source_target_pairs={{0,1},{1,2},{2,3},{4,5},{5,6},{6,7},{8,9},{9,10},{10,11},{12,13},{... | collective-permute-start | bytes 98312 | tf_op jit(solution)/shard_map/while/body/eval_jaxpr/ppermute | solution.py:22
  422.2 7.9 %collective-permute-start.6 = (f32[16,4,128]{2,1,0:T(4,128)S(1)}, f32[16,4,128]{2,1,0:T(4,128)S(1)}, u32[]{:S(2)}, u32[]{:S(2)}) collective-permute-start(f32[16,4,128]{2,1,0:T(4,128)S(1)} %get-tuple-element.662), channel_id=1, source_target_pairs={{0,1},{1,2},{2,3},{4,5},{5,6},{6,7},{8,9},{9,10},{10,11},{12,13},{... | collective-permute-start | bytes 98312 | tf_op jit(solution)/shard_map/while/body/eval_jaxpr/ppermute | solution.py:22
  441.9 7.9 %collective-permute-start.6 = (f32[16,4,128]{2,1,0:T(4,128)S(1)}, f32[16,4,128]{2,1,0:T(4,128)S(1)}, u32[]{:S(2)}, u32[]{:S(2)}) collective-permute-start(f32[16,4,128]{2,1,0:T(4,128)S(1)} %get-tuple-element.662), channel_id=1, source_target_pairs={{0,1},{1,2},{2,3},{4,5},{5,6},{6,7},{8,9},{9,10},{10,11},{12,13},{... | collective-permute-start | bytes 98312 | tf_op jit(solution)/shard_map/while/body/eval_jaxpr/ppermute | solution.py:22
  461.6 7.9 %collective-permute-start.6 = (f32[16,4,128]{2,1,0:T(4,128)S(1)}, f32[16,4,128]{2,1,0:T(4,128)S(1)}, u32[]{:S(2)}, u32[]{:S(2)}) collective-permute-start(f32[16,4,128]{2,1,0:T(4,128)S(1)} %get-tuple-element.662), channel_id=1, source_target_pairs={{0,1},{1,2},{2,3},{4,5},{5,6},{6,7},{8,9},{9,10},{10,11},{12,13},{... | collective-permute-start | bytes 98312 | tf_op jit(solution)/shard_map/while/body/eval_jaxpr/ppermute | solution.py:22
  481.3 7.9 %collective-permute-start.6 = (f32[16,4,128]{2,1,0:T(4,128)S(1)}, f32[16,4,128]{2,1,0:T(4,128)S(1)}, u32[]{:S(2)}, u32[]{:S(2)}) collective-permute-start(f32[16,4,128]{2,1,0:T(4,128)S(1)} %get-tuple-element.662), channel_id=1, source_target_pairs={{0,1},{1,2},{2,3},{4,5},{5,6},{6,7},{8,9},{9,10},{10,11},{12,13},{... | collective-permute-start | bytes 98312 | tf_op jit(solution)/shard_map/while/body/eval_jaxpr/ppermute | solution.py:22
  501.0 7.9 %collective-permute-start.6 = (f32[16,4,128]{2,1,0:T(4,128)S(1)}, f32[16,4,128]{2,1,0:T(4,128)S(1)}, u32[]{:S(2)}, u32[]{:S(2)}) collective-permute-start(f32[16,4,128]{2,1,0:T(4,128)S(1)} %get-tuple-element.662), channel_id=1, source_target_pairs={{0,1},{1,2},{2,3},{4,5},{5,6},{6,7},{8,9},{9,10},{10,11},{12,13},{... | collective-permute-start | bytes 98312 | tf_op jit(solution)/shard_map/while/body/eval_jaxpr/ppermute | solution.py:22
  520.7 7.9 %collective-permute-start.6 = (f32[16,4,128]{2,1,0:T(4,128)S(1)}, f32[16,4,128]{2,1,0:T(4,128)S(1)}, u32[]{:S(2)}, u32[]{:S(2)}) collective-permute-start(f32[16,4,128]{2,1,0:T(4,128)S(1)} %get-tuple-element.662), channel_id=1, source_target_pairs={{0,1},{1,2},{2,3},{4,5},{5,6},{6,7},{8,9},{9,10},{10,11},{12,13},{... | collective-permute-start | bytes 98312 | tf_op jit(solution)/shard_map/while/body/eval_jaxpr/ppermute | solution.py:22
  (91 other events, 1304.8 us)
where the time goes:
time: 539 us; the launch traced here: 532 us
  starting transfers between devices  197 us (37%)
  waiting for transfers between devices  155 us (29%)
  other arithmetic  122 us (23%)
  local copies, waits for them, and re-layouts  46.1 us (9%)
  blocking collectives  7.99 us (1%)
    ppermute x48, waiting for transfers between devices, padded_2(): lax.ppermute(head, axis, [((i + 1) % count, i) for i in range(ends)])  139 us
    ppermute x48, starting transfers between devices, padded_2(): lax.ppermute(tail, axis, [(i, (i + 1) % count) for i in range(ends)])  125 us
    ppermute x48, starting transfers between devices, padded_2(): lax.ppermute(head, axis, [((i + 1) % count, i) for i in range(ends)])  62 us
    scatter-add x24, other arithmetic, place_sum(): jnp.zeros((shape[0] * shape[1] * shape[2],), jnp.float32).at[indices]  49.1 us
    gather x12, local copies, waits for them, and re-layouts, advance(): following.reshape(-1)[cells] * active_flat  37.7 us
    dynamic_update_slice x12, other arithmetic, local(): lax.scan(advance, (state_prev, state_now), source_weight)  29.1 us
    add x12, other arithmetic, retreat(): return ((current, earlier, gradient + earlier * acceleration), None)  21.4 us
    ppermute x48, waiting for transfers between devices, padded_2(): lax.ppermute(tail, axis, [(i, (i + 1) % count) for i in range(ends)])  11.1 us
  transfers between devices with their start and end apart: 98, of which 73 were waited for; matrix products, arithmetic and copies ran while one was open for 27% of the time, Pallas kernels for 0%

commit v1 on v0

--- a/solution.py
+++ b/solution.py
@@ -1,14 +1,660 @@
+import functools
+
 import jax
 import jax.numpy as jnp
 from jax import lax
+from jax.experimental import pallas as pl
+from jax.experimental.pallas import tpu as pltpu
 from jax.sharding import PartitionSpec as P
 
 STEPS = 12
 SPONGE = 8
+REACH = 4
+DEPTH = 4
+LANES = 128
+PAD = 8
 
 
 stencil = (-205.0 / 72.0, 8.0 / 5.0, -1.0 / 5.0, 8.0 / 315.0, -1.0 / 560.0)
 damping_peak = 0.3
+
+
+class Layout:
+    def __init__(self, count_x, count_y, width_x, width_y):
+        self.count_x, self.count_y = count_x, count_y
+        self.width_x, self.width_y = width_x, width_y
+        self.chunk = width_y // count_x
+        self.whole_x = width_x * count_x
+        self.whole_y = width_y * count_y
+        self.margin = REACH * DEPTH
+        self.extent = self.chunk + 2 * self.margin
+        self.stride = self.whole_x + PAD
+        self.padded_rows = self.extent * self.stride + PAD
+        self.kept = self.margin - REACH
+        self.inner = self.extent - 2 * REACH
+
+    def at(self, place):
+        pair, rest = divmod(place, 2 * self.count_x)
+        chip, core = divmod(rest, 2)
+        slab = chip if pair % 2 == 0 else self.count_x - 1 - chip
+        return slab * self.count_y + 2 * pair + core
+
+    def to_chunks(self, turn):
+        moves = []
+        for slab in range(self.count_x):
+            for strip in range(self.count_y):
+                moves.append((slab * self.count_y + strip, self.at(strip * self.count_x + (slab ^ turn))))
+        return moves
+
+    def to_slabs(self, turn):
+        return [(target, source) for source, target in self.to_chunks(turn)]
+
+    def onward(self):
+        last = self.count_x * self.count_y - 1
+        return [(self.at(place), self.at(place + 1)) for place in range(last)]
+
+    def backward(self):
+        return [(target, source) for source, target in self.onward()]
+
+
+def fits(count_x, count_y, width_x, width_y, depth_z):
+    return (
+        count_x & (count_x - 1) == 0
+        and count_y % 2 == 0
+        and width_x == 8
+        and depth_z == LANES
+        and width_y == count_x * REACH * DEPTH
+    )
+
+
+def smem():
+    return pl.BlockSpec(memory_space=pltpu.SMEM)
+
+
+def vmem():
+    return pl.BlockSpec(memory_space=pltpu.VMEM)
+
+
+def f32(*shape):
+    return jax.ShapeDtypeStruct(shape, jnp.float32)
+
+
+def call(kernel, ints, arrays, outs, scratch=(), flops=1_000_000):
+    moved = 4 * (sum(a.size for a in arrays) + sum(o.size for o in outs))
+    return pl.pallas_call(
+        kernel,
+        out_shape=tuple(outs),
+        in_specs=[smem()] * len(ints) + [vmem()] * len(arrays),
+        out_specs=tuple(vmem() for _ in outs),
+        scratch_shapes=list(scratch),
+        compiler_params=pltpu.CompilerParams(vmem_limit_bytes=40 * 1024 * 1024),
+        cost_estimate=pl.CostEstimate(flops=flops, bytes_accessed=moved, transcendentals=0),
+    )(*ints, *arrays)
+
+
+def cut_fields(lay, slab, fields, fill, target, first_row):
+    for turn in range(lay.count_x):
+        start = (slab ^ turn) * lay.chunk
+        row = 0
+        for field in fields:
+            for y in range(lay.chunk):
+                target[turn][row : row + 8, :] = field[pl.ds(start + y, 8, stride=lay.width_y), :]
+                row += 8
+        fill(target[turn], row)
+
+
+def cut_forward(lay, slab_ref, count_ref, now, prev, courant, cell, *sends):
+    slots = lax.broadcasted_iota(jnp.int32, (1, LANES), 1)
+
+    def fill(target, row):
+        for tile in range(lay.count_x):
+            used = jnp.where(slots < count_ref[tile], cell[tile : tile + 1, :], -1)
+            target[row + tile : row + tile + 1, :] = used.astype(jnp.float32)
+
+    cut_fields(lay, slab_ref[0], (now, prev, courant), fill, sends, 0)
+
+
+def cut_adjoint(lay, slab_ref, now, prev, observed, *sends):
+    def fill(target, row):
+        target[row : row + observed.shape[0], :] = observed[...]
+
+    cut_fields(lay, slab_ref[0], (now, prev), fill, sends, 0)
+
+
+def place_rows(lay, ref, layer, start_x, tile):
+    first = pl.multiple_of(layer * lay.whole_x + start_x, 8)
+    ref[pl.ds(first, 8), :] = tile
+
+
+def join_fields(lay, own_slot, pieces, names, state, courant, send_back, send_on):
+    for turn, piece in enumerate(pieces):
+        start_x = pl.multiple_of((own_slot ^ turn) * 8, 8)
+        row = 0
+        for index, name in enumerate(names):
+            first = 0 if index == 0 else lay.chunk + (index - 1) * lay.kept
+            for y in range(lay.chunk):
+                tile = piece[row : row + 8, :]
+                row += 8
+                if name == "courant":
+                    place_rows(lay, courant, y, start_x, tile)
+                else:
+                    place_rows(lay, state, index * lay.chunk + y, start_x, tile)
+                if index == 0:
+                    place_rows(lay, send_back, y, start_x, tile)
+                    place_rows(lay, send_on, y, start_x, tile)
+                    continue
+                if y < lay.kept:
+                    place_rows(lay, send_back, first + y, start_x, tile)
+                if y >= lay.chunk - lay.kept:
+                    place_rows(lay, send_on, first + y - (lay.chunk - lay.kept), start_x, tile)
+
+
+def join_forward(lay, slot_ref, *refs):
+    pieces, (state, courant, send_back, send_on, codes) = refs[: lay.count_x], refs[lay.count_x :]
+    own_slot = slot_ref[0]
+    join_fields(lay, own_slot, pieces, ("now", "prev", "courant"), state, courant, send_back, send_on)
+    first = 3 * lay.chunk * 8
+    strip_cells = lay.width_y * LANES
+    slab_row = lax.broadcasted_iota(jnp.int32, codes.shape, 0)
+    found = jnp.full(codes.shape, -1.0, jnp.float32)
+    for turn, piece in enumerate(pieces):
+        cell = piece[first : first + lay.count_x, :].astype(jnp.int32)
+        used = cell >= 0
+        cell = jnp.maximum(cell, 0)
+        x = lax.div(cell, jnp.int32(strip_cells))
+        y = lax.rem(lax.div(cell, jnp.int32(LANES)), jnp.int32(lay.width_y)) - own_slot * lay.chunk
+        inside = used & (y >= 0) & (y < lay.chunk)
+        code = jnp.where(inside, (y * 8 + x) * LANES + lax.rem(cell, jnp.int32(LANES)), -1)
+        code = code.astype(jnp.float32)
+        line = jnp.concatenate([code[tile : tile + 1, :] for tile in range(lay.count_x)], axis=1)
+        found = jnp.where(slab_row == (own_slot ^ turn), jnp.broadcast_to(line, codes.shape), found)
+    codes[...] = found
+
+
+def join_adjoint(lay, slot_ref, *refs):
+    pieces, (state, send_back, send_on) = refs[: lay.count_x], refs[lay.count_x :]
+    join_fields(lay, slot_ref[0], pieces, ("now", "prev"), state, None, send_back, send_on)
+
+
+def zero_pads(lay, buffers):
+    zeros = jnp.zeros((PAD, LANES), jnp.float32)
+    for y in range(lay.extent + 1):
+        for buffer in buffers:
+            buffer[y * lay.stride : y * lay.stride + PAD, :] = zeros
+
+
+def load_state(lay, now, prev, state, from_back, from_on):
+    wide, own = lay.whole_x, lay.margin
+
+    def put(buffer, layer, ref, source):
+        first = layer * lay.stride + PAD
+        buffer[first : first + wide, :] = ref[source * wide : (source + 1) * wide, :]
+
+    for y in range(lay.chunk):
+        put(now, own + y, state, y)
+        put(prev, own + y, state, lay.chunk + y)
+        put(now, y, from_back, y)
+        put(now, own + lay.chunk + y, from_on, y)
+    for y in range(lay.kept):
+        put(prev, REACH + y, from_back, lay.chunk + y)
+        put(prev, own + lay.chunk + y, from_on, lay.chunk + y)
+
+
+def store_state(lay, now, prev, state, send_back, send_on):
+    wide, own = lay.whole_x, lay.margin
+    skipped = lay.chunk - lay.kept
+
+    def put(ref, target, values):
+        ref[target * wide : (target + 1) * wide, :] = values
+
+    for y in range(lay.chunk):
+        first = (own + y) * lay.stride + PAD
+        values = now[first : first + wide, :]
+        put(state, y, values)
+        put(send_back, y, values)
+        put(send_on, y, values)
+        values = prev[first : first + wide, :]
+        put(state, lay.chunk + y, values)
+        if y < lay.kept:
+            put(send_back, lay.chunk + y, values)
+        if y >= skipped:
+            put(send_on, lay.chunk + y - skipped, values)
+
+
+def fill_gain(lay, first_y, gain):
+    x = lax.broadcasted_iota(jnp.int32, (lay.whole_x, LANES), 0)
+    gap_x = jnp.minimum(x, lay.whole_x - 1 - x)
+    ramp_x = jnp.maximum(SPONGE - gap_x, 0).astype(jnp.float32) / SPONGE
+    part_x = ramp_x * ramp_x
+
+    def layer(y, carry):
+        global_y = jnp.full((lay.whole_x, LANES), first_y + REACH + y, jnp.int32)
+        gap_y = jnp.minimum(global_y, lay.whole_y - 1 - global_y)
+        ramp_y = jnp.maximum(SPONGE - gap_y, 0).astype(jnp.float32) / SPONGE
+        first = pl.multiple_of(y * lay.whole_x, 8)
+        gain[pl.ds(first, lay.whole_x), :] = 2.0 / (1.0 + damping_peak * (part_x + ramp_y * ramp_y))
+        return carry
+
+    lax.fori_loop(0, lay.inner, layer, 0)
+
+
+def sweep(lay, step, now, prev, following, courant, gain, inject=None):
+    wide, stride = lay.whole_x, lay.stride
+    first_layer = REACH * (step + 1)
+    group = 8
+    z = lax.broadcasted_iota(jnp.int32, (wide, LANES), 1)
+    up = [jnp.where(z >= k, stencil[k], 0.0).astype(jnp.float32) for k in range(REACH + 1)]
+    down = [jnp.where(z < LANES - k, stencil[k], 0.0).astype(jnp.float32) for k in range(REACH + 1)]
+
+    def layers(block, carry):
+        for inner in range(group):
+            y = first_layer + group * block + inner
+            base = pl.multiple_of(y * stride + PAD, 8)
+            flat = pl.multiple_of((y - REACH) * wide, 8)
+            center = now[pl.ds(base, wide), :]
+            total = (3.0 * stencil[0]) * center
+            for k in range(1, REACH + 1):
+                pair = now[pl.ds(base + k, wide), :] + now[pl.ds(base - k, wide), :]
+                pair = pair + (now[pl.ds(base + stride * k, wide), :] + now[pl.ds(base - stride * k, wide), :])
+                total = total + stencil[k] * pair
+                total = total + up[k] * pltpu.roll(center, k, 1)
+                total = total + down[k] * pltpu.roll(center, LANES - k, 1)
+            if inject is not None:
+                total = total + inject[step, pl.ds(flat, wide), :]
+            former = prev[pl.ds(base, wide), :]
+            change = (center - former) + (0.5 * courant[pl.ds(flat, wide), :]) * total
+            following[pl.ds(base, wide), :] = former + gain[pl.ds(flat, wide), :] * change
+        return carry
+
+    lax.fori_loop(0, (lay.extent - 2 * first_layer) // group, layers, 0)
+
+
+def split(values):
+    high = values.astype(jnp.bfloat16)
+    rest = values - high.astype(jnp.float32)
+    middle = rest.astype(jnp.bfloat16)
+    low = (rest - middle.astype(jnp.float32)).astype(jnp.bfloat16)
+    return high, middle, low
+
+
+def slot_rows(codes, slab):
+    code = codes[slab : slab + 1, :].astype(jnp.int32)
+    row = jnp.where(code >= 0, lax.shift_right_arithmetic(code, 7), -1)
+    return row, jnp.where(code >= 0, code & (LANES - 1), -1)
+
+
+def forward(lay, phase, sources, ints, wavelet, state, from_back, from_on, courant_in, codes, *refs):
+    first, last = phase == 0, phase == STEPS // DEPTH - 1
+    rows = lay.chunk * lay.whole_x
+    refs = list(refs)
+    earlier, observed = [], []
+    if last:
+        earlier = [refs.pop(0) for _ in range(phase)]
+        observed = [refs.pop(0) for _ in range(lay.count_x)]
+    accel = refs.pop(0)
+    if first:
+        courant = refs.pop(0)
+    else:
+        courant = courant_in
+    if last:
+        misfit = refs.pop(0)
+    else:
+        state_out, send_back, send_on, record = [refs.pop(0) for _ in range(4)]
+    buffers = [refs.pop(0) for _ in range(3)]
+    gain, pulse, stash = refs.pop(0), refs.pop(0), refs.pop(0)
+    if last:
+        record = refs.pop(0)
+    now, prev, following = buffers
+
+    zero_pads(lay, buffers)
+    load_state(lay, now, prev, state, from_back, from_on)
+    if first:
+        tail = (lay.chunk + lay.kept) * lay.whole_x
+        part = lay.kept * lay.whole_x
+        courant[0:part, :] = from_back[tail : tail + part, :]
+        courant[part : part + rows, :] = courant_in[...]
+        courant[part + rows : part + rows + part, :] = from_on[tail : tail + part, :]
+    fill_gain(lay, ints[0], gain)
+    lane = lax.broadcasted_iota(jnp.int32, (1, LANES), 1)
+    for source in range(sources):
+        flat = pl.ds(ints[1 + sources + source], 1)
+        strength = 0.5 * courant[flat, :] * gain[flat, :]
+        pulse[source : source + 1, :] = jnp.where(lane == ints[1 + 2 * sources + source], strength, 0.0)
+
+    for step in range(DEPTH):
+        sweep(lay, step, now, prev, following, courant, gain)
+        for source in range(sources):
+            row = pl.ds(ints[1 + source], 1)
+            weight = wavelet[phase * DEPTH + step, source]
+            following[row, :] = following[row, :] + weight * pulse[source : source + 1, :]
+
+        def own_layers(index, carry):
+            pair = []
+            for y in (2 * index, 2 * index + 1):
+                base = pl.multiple_of((lay.margin + y) * lay.stride + PAD, 8)
+                later, center = following[pl.ds(base, lay.whole_x), :], now[pl.ds(base, lay.whole_x), :]
+                change = (later - center) - (center - prev[pl.ds(base, lay.whole_x), :])
+                target = pl.multiple_of((step * lay.chunk + y) * lay.whole_x, 8)
+                accel[pl.ds(target, lay.whole_x), :] = change
+                pair.append(later)
+            for slab in range(lay.count_x):
+                both = jnp.concatenate([part[slab * 8 : slab * 8 + 8, :] for part in pair], axis=0)
+                target = pl.multiple_of((slab * DEPTH + step) * lay.chunk * 8 + index * 16, 16)
+                for place, values in enumerate(split(both)):
+                    stash[pl.ds(target, 16), place * LANES : (place + 1) * LANES] = values
+            return carry
+
+        lax.fori_loop(0, lay.chunk // 2, own_layers, 0)
+        now, prev, following = following, now, prev
+
+    slots = codes.shape[1]
+    cells = lay.chunk * 8
+    width = 2 * LANES
+    for slab in range(lay.count_x):
+        cell_row, cell_z = slot_rows(codes, slab)
+        for start in range(0, slots, width):
+            here = slice(start, start + width)
+            z = lax.broadcasted_iota(jnp.int32, (LANES, width), 0)
+            pick = jnp.where(z == cell_z[:, here], 1.0, 0.0).astype(jnp.bfloat16)
+            pick = jnp.concatenate([pick] * 3, axis=0)
+            found = jnp.dot(
+                stash[slab * DEPTH * cells : (slab + 1) * DEPTH * cells, :],
+                pick,
+                preferred_element_type=jnp.float32,
+            )
+            wanted = lax.broadcasted_iota(jnp.int32, (cells, width), 0) == cell_row[:, here]
+            for step in range(DEPTH):
+                part = jnp.where(wanted, found[step * cells : (step + 1) * cells, :], 0.0)
+                row = step * lay.count_x + slab
+                record[row : row + 1, here] = jnp.sum(part, axis=0, keepdims=True)
+
+    if not last:
+        store_state(lay, now, prev, state_out, send_back, send_on)
+        return
+    block = DEPTH * lay.count_x
+    for index, part in enumerate(earlier + [record]):
+        misfit[index * block : (index + 1) * block, :] = part[...]
+    total = STEPS * lay.count_x
+    for slab in range(lay.count_x):
+        misfit[total + slab : total + slab + 1, :] = codes[slab : slab + 1, :]
+    own_slot = ints[1 + 3 * sources]
+    for turn, piece in enumerate(observed):
+        place = pl.ds(pl.multiple_of((own_slot ^ turn) * LANES, LANES), LANES)
+        used = jnp.concatenate([codes[:, place]] * STEPS, axis=0) >= 0
+        seen = piece[2 * lay.chunk * 8 : 2 * lay.chunk * 8 + total, :]
+        misfit[0:total, place] = jnp.where(used, misfit[0:total, place] - seen, 0.0)
+
+
+def spread(lay, phase, misfits, inject):
+    cells = lay.chunk * 8
+    for slab in range(lay.count_x):
+        for side, misfit in zip((-1, 0, 1), misfits):
+            codes = misfit[STEPS * lay.count_x : (STEPS + 1) * lay.count_x, :]
+            cell_row, cell_z = slot_rows(codes, slab)
+            slots = cell_row.shape[1]
+            z = lax.broadcasted_iota(jnp.int32, (LANES, slots), 0)
+            pick = jnp.where(z == cell_z, 1.0, 0.0).astype(jnp.bfloat16)
+            pick = jnp.concatenate([pick] * 3, axis=1)
+            hit = lax.broadcasted_iota(jnp.int32, (cells, slots), 0) == cell_row
+            hit = jnp.where(hit, 1.0, 0.0).astype(jnp.bfloat16)
+            left, spans = [], []
+            for step in range(DEPTH):
+                low, high = 0, lay.chunk
+                if side < 0:
+                    low = REACH * (step + 1) - lay.margin + lay.chunk
+                if side > 0:
+                    high = lay.margin - REACH * (step + 1)
+                if low >= high:
+                    continue
+                moment = STEPS - 1 - phase * DEPTH - step
+                row = moment * lay.count_x + slab
+                parts = split(misfit[row : row + 1, :])
+                left.append(jnp.concatenate([hit[low * 8 : high * 8, :] * part for part in parts], axis=1))
+                spans.append((step, low, high))
+            placed = lax.dot_general(
+                jnp.concatenate(left, axis=0),
+                pick,
+                (((1,), (1,)), ((), ())),
+                preferred_element_type=jnp.float32,
+            )
+            at = 0
+            for step, low, high in spans:
+                for y in range(low, high):
+                    layer = lay.margin + side * lay.chunk + y - REACH
+                    target = layer * lay.whole_x + slab * 8
+                    inject[step, target : target + 8, :] = placed[at : at + 8, :]
+                    at += 8
+
+
+def backward(lay, phase, ints, state, from_back, from_on, courant, accel, misfit, misfit_back, misfit_on, *refs):
+    first, last = phase == 0, phase == STEPS // DEPTH - 1
+    refs = list(refs)
+    if not first:
+        gradient_in = refs.pop(0)
+    if last:
+        sends = [refs.pop(0) for _ in range(lay.count_x)]
+    else:
+        gradient, state_out, send_back, send_on = [refs.pop(0) for _ in range(4)]
+    buffers = [refs.pop(0) for _ in range(3)]
+    gain, inject = refs.pop(0), refs.pop(0)
+    if last:
+        gradient = refs.pop(0)
+    now, prev, following = buffers
+
+    zero_pads(lay, buffers)
+    load_state(lay, now, prev, state, from_back, from_on)
+    fill_gain(lay, ints[0], gain)
+    spread(lay, phase, (misfit_back, misfit, misfit_on), inject)
+    for step in range(DEPTH):
+        sweep(lay, step, now, prev, following, courant, gain, inject)
+
+        def own_layers(y, carry):
+            base = pl.multiple_of((lay.margin + y) * lay.stride + PAD, 8)
+            source = pl.multiple_of(((DEPTH - 1 - step) * lay.chunk + y) * lay.whole_x, 8)
+            target = pl.ds(pl.multiple_of(y * lay.whole_x, 8), lay.whole_x)
+            term = following[pl.ds(base, lay.whole_x), :] * accel[pl.ds(source, lay.whole_x), :]
+            if step > 0:
+                term = gradient[target, :] + term
+            elif not first:
+                term = gradient_in[target, :] + term
+            gradient[target, :] = term
+            return carry
+
+        lax.fori_loop(0, lay.chunk, own_layers, 0)
+        now, prev, following = following, now, prev
+
+    if not last:
+        store_state(lay, now, prev, state_out, send_back, send_on)
+        return
+    own_slot = ints[1]
+    total = STEPS * lay.count_x
+    for turn, send in enumerate(sends):
+        other = own_slot ^ turn
+        for y in range(lay.chunk):
+            source = pl.ds(pl.multiple_of(y * lay.whole_x + other * 8, 8), 8)
+            send[y * 8 : y * 8 + 8, :] = gradient[source, :]
+        tile = pl.ds(pl.multiple_of(other * LANES, LANES), LANES)
+        send[lay.chunk * 8 : lay.chunk * 8 + total, :] = misfit[0:total, tile]
+
+
+def finish(lay, slab_ref, *refs):
+    pieces, (gradient, residual) = refs[: lay.count_x], refs[lay.count_x :]
+    slab = slab_ref[0]
+    total = None
+    for turn, piece in enumerate(pieces):
+        start = (slab ^ turn) * lay.chunk
+        for x in range(8):
+            target = pl.ds(pl.multiple_of(x * lay.width_y + start, 8), lay.chunk)
+            gradient[target, :] = piece[pl.ds(x, lay.chunk, stride=8), :]
+        part = piece[lay.chunk * 8 : lay.chunk * 8 + residual.shape[0], :]
+        total = part if total is None else total + part
+    residual[...] = total
+
+
+def local_tiles(
+    lay,
+    courant,
+    state_prev,
+    state_now,
+    adjoint_now,
+    adjoint_next,
+    source_cell,
+    wavelet,
+    observed,
+    receiver_cell,
+    receiver_count,
+):
+    axes = ("gx", "gy")
+    slab = lax.axis_index("gx")
+    strip = lax.axis_index("gy")
+    pair = strip // 2
+    chip = jnp.where(pair % 2 == 0, slab, lay.count_x - 1 - slab)
+    place = (pair * lay.count_x + chip) * 2 + strip % 2
+    own_slot = place % lay.count_x
+    first_y = place * lay.chunk - lay.margin
+    slab_int = slab.reshape(1).astype(jnp.int32)
+    slot_int = own_slot.reshape(1).astype(jnp.int32)
+
+    count = lay.count_x
+    wide = lay.whole_x
+    rows = lay.chunk * wide
+    cells = lay.chunk * 8
+    sources = source_cell.shape[0]
+    slots = count * receiver_cell.shape[3]
+    flat = lambda values: values.reshape(-1, LANES)
+
+    source_x = source_cell // (lay.whole_y * LANES)
+    source_y = source_cell // LANES % lay.whole_y - first_y
+    source_z = source_cell % LANES
+    inside = (source_y >= REACH) & (source_y < lay.extent - REACH)
+    source_row = jnp.where(inside, source_y * lay.stride + PAD + source_x, REACH * lay.stride + PAD)
+    source_flat = jnp.where(inside, (source_y - REACH) * wide + source_x, 0)
+    source_z = jnp.where(inside, source_z, -1)
+    ints = jnp.concatenate(
+        [first_y.reshape(1), source_row, source_flat, source_z, own_slot.reshape(1)]
+    ).astype(jnp.int32)
+    back_ints = jnp.stack([first_y, own_slot]).astype(jnp.int32)
+
+    def exchange(send_back, send_on):
+        return (
+            lax.ppermute(send_on, axes, lay.onward()),
+            lax.ppermute(send_back, axes, lay.backward()),
+        )
+
+    tail = -(-count // 8) * 8
+    cuts = call(
+        functools.partial(cut_forward, lay),
+        (slab_int, receiver_count.reshape(-1)),
+        (flat(state_now), flat(state_prev), flat(courant), receiver_cell.reshape(count, LANES)),
+        [f32(3 * cells + tail, LANES)] * count,
+    )
+    pieces = [lax.ppermute(cut, axes, lay.to_chunks(turn)) for turn, cut in enumerate(cuts)]
+    kept_rows = lay.kept * wide
+    state, own_courant, send_back, send_on, codes = call(
+        functools.partial(join_forward, lay),
+        (slot_int,),
+        pieces,
+        [f32(2 * rows, LANES), f32(rows, LANES)]
+        + [f32(rows + 2 * kept_rows, LANES)] * 2
+        + [f32(count, slots)],
+    )
+    from_back, from_on = exchange(send_back, send_on)
+
+    traces = flat(observed)
+    cuts = call(
+        functools.partial(cut_adjoint, lay),
+        (slab_int,),
+        (flat(adjoint_now), flat(adjoint_next), traces),
+        [f32(2 * cells + traces.shape[0], LANES)] * count,
+    )
+    back_pieces = [lax.ppermute(cut, axes, lay.to_chunks(turn)) for turn, cut in enumerate(cuts)]
+    state_shapes = [f32(2 * rows, LANES)] + [f32(rows + kept_rows, LANES)] * 2
+    back_state, back_send_back, back_send_on = call(
+        functools.partial(join_adjoint, lay), (slot_int,), back_pieces, state_shapes
+    )
+    back_from_back, back_from_on = exchange(back_send_back, back_send_on)
+
+    phases = STEPS // DEPTH
+    block = DEPTH * count
+    buffers = [pltpu.VMEM((lay.padded_rows, LANES), jnp.float32)] * 3
+    inner = lay.inner * wide
+    gain = pltpu.VMEM((inner, LANES), jnp.float32)
+    accels, records = [], []
+    courant_all = own_courant
+    for phase in range(phases):
+        first, last = phase == 0, phase == phases - 1
+        arrays = [state, from_back, from_on, courant_all, codes]
+        outs = [f32(DEPTH * rows, LANES)]
+        scratch = buffers + [
+            gain,
+            pltpu.VMEM((sources, LANES), jnp.float32),
+            pltpu.VMEM((count * DEPTH * cells, 3 * LANES), jnp.bfloat16),
+        ]
+        if first:
+            outs.append(f32(inner, LANES))
+        if last:
+            arrays += records + back_pieces
+            outs.append(f32(-(-(STEPS + 1) * count // 8) * 8, slots))
+            scratch.append(pltpu.VMEM((block, slots), jnp.float32))
+        else:
+            outs += state_shapes + [f32(block, slots)]
+        results = list(
+            call(
+                functools.partial(forward, lay, phase, sources),
+                (ints, wavelet),
+                arrays,
+                outs,
+                scratch,
+                flops=20_000_000,
+            )
+        )
+        accels.append(results.pop(0))
+        if first:
+            courant_all = results.pop(0)
+        if last:
+            misfit = results.pop(0)
+        else:
+            state, send_back, send_on, record = results
+            records.append(record)
+            from_back, from_on = exchange(send_back, send_on)
+
+    misfit_back, misfit_on = exchange(misfit, misfit)
+    state, from_back, from_on = back_state, back_from_back, back_from_on
+    gradient = None
+    for phase in range(phases):
+        first, last = phase == 0, phase == phases - 1
+        arrays = [state, from_back, from_on, courant_all, accels[phases - 1 - phase]]
+        arrays += [misfit, misfit_back, misfit_on]
+        scratch = buffers + [gain, pltpu.VMEM((DEPTH, inner, LANES), jnp.float32)]
+        if not first:
+            arrays.append(gradient)
+        if last:
+            outs = [f32(cells + traces.shape[0], LANES)] * count
+            scratch.append(pltpu.VMEM((rows, LANES), jnp.float32))
+        else:
+            outs = [f32(rows, LANES)] + state_shapes
+        results = call(
+            functools.partial(backward, lay, phase), (back_ints,), arrays, outs, scratch, flops=20_000_000
+        )
+        if not last:
+            gradient, state, send_back, send_on = results
+            from_back, from_on = exchange(send_back, send_on)
+    pieces = [lax.ppermute(send, axes, lay.to_slabs(turn)) for turn, send in enumerate(results)]
+    gradient, residual = call(
+        functools.partial(finish, lay),
+        (slab_int,),
+        pieces,
+        [f32(lay.width_x * lay.width_y, LANES), f32(*traces.shape)],
+    )
+    return gradient.reshape(courant.shape), residual.reshape(observed.shape)
+
+
+def local(courant, *rest):
+    width_x, width_y, depth_z = courant.shape
+    count_x, count_y = lax.axis_size("gx"), lax.axis_size("gy")
+    if fits(count_x, count_y, width_x, width_y, depth_z):
+        return local_tiles(Layout(count_x, count_y, width_x, width_y), courant, *rest)
+    return local_blocks(courant, *rest)
 
 
 def padded_2(cells, sides, width):
@@ -64,7 +710,7 @@
     return flat.reshape(shape)
 
 
-def local(
+def local_blocks(
     courant,
     state_prev,
     state_now,

time: 539 us -> 181 us (0.34)
  waiting for transfers between devices: 155 us -> 27.1 us
  other arithmetic: 122 us -> 0.12 us
  starting transfers between devices: 197 us -> 84.6 us
  Pallas kernels: 0 us -> 62 us
  local copies, waits for them, and re-layouts: 46.1 us -> 3.63 us
  blocking collectives: 7.99 us -> 0 us
    ppermute x96 -> x26, waiting for transfers between devices: 150 us -> 27.1 us  [the longest x8 13.6 us: local_tiles(): lax.ppermute(cut, axes, lay.to_chunks(turn))]
    ppermute x96 -> x26, starting transfers between devices: 187 us -> 84.6 us  [the longest x7 40.7 us: exchange(): lax.ppermute(send_on, axes, lay.onward())]
    pallas_call x0 -> x11, Pallas kernels: none -> 62 us  [call(): pl.pallas_call(kernel, out_shape=tuple(outs), in_specs=[smem()] * len(int...]
    scatter-add x24 -> x0, other arithmetic: 49.1 us -> none  [place_sum(): jnp.zeros((shape[0] * shape[1] * shape[2],), jnp.float32).at[indices]]
    gather x12 -> x0, local copies, waits for them, and re-layouts: 37.7 us -> none  [advance(): following.reshape(-1)[cells] * active_flat]
    dynamic_update_slice x12 -> x0, other arithmetic: 29.1 us -> none  [local(): lax.scan(advance, (state_prev, state_now), source_weight)]
    add x12 -> x0, other arithmetic: 21.4 us -> none  [retreat(): return ((current, earlier, gradient + earlier * acceleration), None)]
    select_n x37 -> x3, other arithmetic: 17.2 us -> 0.04 us  [the longest x1 0.02 us: local_tiles(): source_z = jnp.where(inside, source_z, -1)]
  transfers between devices with their start and end apart: 98 -> 26, of which waited for: 73 -> 10; matrix products, arithmetic and copies ran while one was open for 27% -> 0% of each run, Pallas kernels for 0% -> 11%
where the time goes in v1:
time: 181 us; the launch traced here: 179 us
  starting transfers between devices  84.6 us (47%)
  Pallas kernels  62 us (34%)
  waiting for transfers between devices  27.1 us (15%)
  local copies, waits for them, and re-layouts  3.63 us (2%)
    pallas_call x11, Pallas kernels, call(): pl.pallas_call(kernel, out_shape=tuple(outs), in_specs=[smem()] * len(int...  62 us
    ppermute x7, starting transfers between devices, exchange(): lax.ppermute(send_on, axes, lay.onward())  40.7 us
    ppermute x8, starting transfers between devices, local_tiles(): lax.ppermute(cut, axes, lay.to_chunks(turn))  17.4 us
    ppermute x4, starting transfers between devices, local_tiles(): lax.ppermute(send, axes, lay.to_slabs(turn))  17.3 us
    ppermute x8, waiting for transfers between devices, local_tiles(): lax.ppermute(cut, axes, lay.to_chunks(turn))  13.6 us
    ppermute x7, starting transfers between devices, exchange(): lax.ppermute(send_back, axes, lay.backward())  9.27 us
    ppermute x7, waiting for transfers between devices, exchange(): lax.ppermute(send_back, axes, lay.backward())  8.73 us
    ppermute x4, waiting for transfers between devices, local_tiles(): lax.ppermute(send, axes, lay.to_slabs(turn))  3.78 us
  transfers between devices with their start and end apart: 26, of which 10 were waited for; matrix products, arithmetic and copies ran while one was open for 0% of the time, Pallas kernels for 11%

profile of v1, /device:TPU:0, one launch (start us, length us, event | category | flops | bytes accessed | tf_op | source)
XLA Modules:
  0.0 178.6 jit_solution(12235505414670905487)
XLA Ops:
  5.9 5.4 %collective-permute-start.7 = (f32[392,128]{1,0:T(8,128)S(1)}, f32[392,128]{1,0:T(8,128)S(1)}, u32[]{:S(2)}, u32[]{:S(2)}) collective-permute-start(f32[392,128]{1,0:T(8,128)S(1)} %get-tuple-element.53), channel_id=1, source_target_pairs={{0,1},{1,9},{2,15},{3,7},{4,0},{5,8},{6,14},{7,6},{8,5},{9,13},{10... | collective-permute-start | bytes 602120 | tf_op jit(solution)/shard_map/ppermute | solution.py:551
  11.3 3.2 %collective-permute-start.9 = (f32[392,128]{1,0:T(8,128)S(1)}, f32[392,128]{1,0:T(8,128)S(1)}, u32[]{:S(2)}, u32[]{:S(2)}) collective-permute-start(f32[392,128]{1,0:T(8,128)S(1)} %get-tuple-element.55), channel_id=1, source_target_pairs={{0,5},{1,13},{2,11},{3,3},{4,4},{5,12},{6,10},{7,2},{8,1},{9,9},{1... | collective-permute-start | bytes 602120 | tf_op jit(solution)/shard_map/ppermute | solution.py:551
  16.0 12.2 %collective-permute-done.8.refs_2_ = f32[392,128]{1,0:T(8,128)S(1)} collective-permute-done((f32[392,128]{1,0:T(8,128)S(1)}, f32[392,128]{1,0:T(8,128)S(1)}, u32[]{:S(2)}, u32[]{:S(2)}) %collective-permute-start.8) | collective-permute-done | bytes 200736 | tf_op jit(solution)/shard_map/ppermute | solution.py:551
  28.4 3.9 %collective-permute-start.10 = (f32[1280,128]{1,0:T(8,128)S(1)}, f32[1280,128]{1,0:T(8,128)S(1)}, u32[]{:S(2)}, u32[]{:S(2)}) collective-permute-start(f32[1280,128]{1,0:T(8,128)S(1)} %get-tuple-element.57), channel_id=1, source_target_pairs={{0,1},{1,4},{4,5},{5,8},{8,9},{9,12},{12,13},{13,14},{14,15},{15,1... | collective-permute-start | bytes 1966088 | tf_op jit(solution)/shard_map/ppermute | solution.py:540
  34.0 2.3 %collective-permute-done.11.from_on = f32[1280,128]{1,0:T(8,128)S(1)} collective-permute-done((f32[1280,128]{1,0:T(8,128)S(1)}, f32[1280,128]{1,0:T(8,128)S(1)}, u32[]{:S(2)}, u32[]{:S(2)}) %collective-permute-start.11) | collective-permute-done | bytes 655392 | tf_op jit(solution)/shard_map/ppermute | solution.py:541
  36.3 9.4 %shard_map.117 = (f32[2048,128]{1,0:T(8,128)S(1)}, f32[1280,128]{1,0:T(8,128)S(1)}, f32[1024,128]{1,0:T(8,128)S(1)}, f32[896,128]{1,0:T(8,128)S(1)}, f32[896,128]{1,0:T(8,128)S(1)}, /*index=5*/f32[16,512]{1,0:T(8,128)S(1)}) custom-call(s32[50]{0:T(128)S(1)} %concatenate.3.ints, f32[12,16]{1,0:T(8,128)S(1)} %copy-done.5, ...), custom_call_target="tpu_custom_call" | custom-call | flops 20000000 | bytes 5283840 | tf_op jit(solution)/shard_map/pallas_call | solution.py:84
  45.7 9.8 %collective-permute-start.12 = (f32[896,128]{1,0:T(8,128)S(1)}, f32[896,128]{1,0:T(8,128)S(1)}, u32[]{:S(2)}, u32[]{:S(2)}) collective-permute-start(f32[896,128]{1,0:T(8,128)S(1)} %get-tuple-element.63), channel_id=1, source_target_pairs={{0,1},{1,4},{4,5},{5,8},{8,9},{9,12},{12,13},{13,14},{14,15},{15,1... | collective-permute-start | bytes 1376264 | tf_op jit(solution)/shard_map/ppermute | solution.py:540
  57.8 4.1 %collective-permute-start.1 = (f32[304,128]{1,0:T(8,128)S(1)}, f32[304,128]{1,0:T(8,128)S(1)}, u32[]{:S(2)}, u32[]{:S(2)}) collective-permute-start(f32[304,128]{1,0:T(8,128)S(1)} %get-tuple-element.46), channel_id=1, source_target_pairs={{0,1},{1,9},{2,15},{3,7},{4,0},{5,8},{6,14},{7,6},{8,5},{9,13},{10... | collective-permute-start | bytes 466952 | tf_op jit(solution)/shard_map/ppermute | solution.py:570
  62.0 3.3 %collective-permute-start.3 = (f32[304,128]{1,0:T(8,128)S(1)}, f32[304,128]{1,0:T(8,128)S(1)}, u32[]{:S(2)}, u32[]{:S(2)}) collective-permute-start(f32[304,128]{1,0:T(8,128)S(1)} %get-tuple-element.48), channel_id=1, source_target_pairs={{0,5},{1,13},{2,11},{3,3},{4,4},{5,12},{6,10},{7,2},{8,1},{9,9},{1... | collective-permute-start | bytes 466952 | tf_op jit(solution)/shard_map/ppermute | solution.py:570
  65.2 9.3 %shard_map.118 = (f32[2048,128]{1,0:T(8,128)S(1)}, f32[1024,128]{1,0:T(8,128)S(1)}, f32[896,128]{1,0:T(8,128)S(1)}, f32[896,128]{1,0:T(8,128)S(1)}, f32[16,512]{1,0:T(8,128)S(1)}) custom-call(s32[50]{0:T(128)S(1)} %concatenate.3.ints, f32[12,16]{1,0:T(8,128)S(1)} %copy-done.5, f32[1024,128]{1,0:T(8,128)S(1)} %get-tuple-element.62.state, ...), custom_call_target="tpu_custom_call" | custom-call | flops 20000000 | bytes 4628480 | tf_op jit(solution)/shard_map/pallas_call | solution.py:84
  74.5 3.2 %collective-permute-start.14 = (f32[896,128]{1,0:T(8,128)S(1)}, f32[896,128]{1,0:T(8,128)S(1)}, u32[]{:S(2)}, u32[]{:S(2)}) collective-permute-start(f32[896,128]{1,0:T(8,128)S(1)} %get-tuple-element.66), channel_id=1, source_target_pairs={{0,1},{1,4},{4,5},{5,8},{8,9},{9,12},{12,13},{13,14},{14,15},{15,1... | collective-permute-start | bytes 1376264 | tf_op jit(solution)/shard_map/ppermute | solution.py:540
  79.2 3.1 %collective-permute-start.4 = (f32[896,128]{1,0:T(8,128)S(1)}, f32[896,128]{1,0:T(8,128)S(1)}, u32[]{:S(2)}, u32[]{:S(2)}) collective-permute-start(f32[896,128]{1,0:T(8,128)S(1)} %get-tuple-element.50), channel_id=1, source_target_pairs={{0,1},{1,4},{4,5},{5,8},{8,9},{9,12},{12,13},{13,14},{14,15},{15,1... | collective-permute-start | bytes 1376264 | tf_op jit(solution)/shard_map/ppermute | solution.py:540
  83.6 9.2 %shard_map.119 = (f32[2048,128]{1,0:T(8,128)S(1)}, f32[56,512]{1,0:T(8,128)S(1)}) custom-call(s32[50]{0:T(128)S(1)} %concatenate.3.ints, f32[12,16]{1,0:T(8,128)S(1)} %copy-done.5, f32[1024,128]{1,0:T(8,128)S(1)} %get-tuple-element.65.state, f32[896,128]{1,0:T(8,128)S(1)} %collective-permute-done.14.from_back, ...), custom_call_target="tpu_custom_call" | custom-call | flops 20000000 | bytes 3956736 | tf_op jit(solution)/shard_map/pallas_call | solution.py:84
  94.2 7.8 %collective-permute-start.16 = (f32[56,512]{1,0:T(8,128)S(1)}, f32[56,512]{1,0:T(8,128)S(1)}, u32[]{:S(2)}, u32[]{:S(2)}) collective-permute-start(f32[56,512]{1,0:T(8,128)S(1)} %get-tuple-element.71.misfit), channel_id=1, source_target_pairs={{0,1},{1,4},{4,5},{5,8},{8,9},{9,12},{12,13},{13,14},{14,15},{15,1... | collective-permute-start | bytes 344072 | tf_op jit(solution)/shard_map/ppermute | solution.py:540
  102.7 10.6 %shard_map.120 = (f32[512,128]{1,0:T(8,128)S(1)}, f32[1024,128]{1,0:T(8,128)S(1)}, f32[896,128]{1,0:T(8,128)S(1)}, f32[896,128]{1,0:T(8,128)S(1)}) custom-call(s32[2]{0:T(128)S(1)} %pad_add_fusion.ints, f32[1024,128]{1,0:T(8,128)S(1)} %get-tuple-element.49.state, f32[896,128]{1,0:T(8,128)S(1)} %collective-permute-done.4.from_back, ...), custom_call_target="tpu_custom_call" | custom-call | flops 20000000 | bytes 5193728 | tf_op jit(solution)/shard_map/pallas_call | solution.py:84
  113.3 4.5 %collective-permute-start.18 = (f32[896,128]{1,0:T(8,128)S(1)}, f32[896,128]{1,0:T(8,128)S(1)}, u32[]{:S(2)}, u32[]{:S(2)}) collective-permute-start(f32[896,128]{1,0:T(8,128)S(1)} %get-tuple-element.73), channel_id=1, source_target_pairs={{0,1},{1,4},{4,5},{5,8},{8,9},{9,12},{12,13},{13,14},{14,15},{15,1... | collective-permute-start | bytes 1376264 | tf_op jit(solution)/shard_map/ppermute | solution.py:540
  119.2 4.2 %collective-permute-done.19.from_on = f32[896,128]{1,0:T(8,128)S(1)} collective-permute-done((f32[896,128]{1,0:T(8,128)S(1)}, f32[896,128]{1,0:T(8,128)S(1)}, u32[]{:S(2)}, u32[]{:S(2)}) %collective-permute-start.19) | collective-permute-done | bytes 458784 | tf_op jit(solution)/shard_map/ppermute | solution.py:541
  123.4 10.6 %shard_map.121 = (f32[512,128]{1,0:T(8,128)S(1)}, f32[1024,128]{1,0:T(8,128)S(1)}, f32[896,128]{1,0:T(8,128)S(1)}, f32[896,128]{1,0:T(8,128)S(1)}) custom-call(s32[2]{0:T(128)S(1)} %pad_add_fusion.ints, f32[1024,128]{1,0:T(8,128)S(1)} %get-tuple-element.72.state, f32[896,128]{1,0:T(8,128)S(1)} %collective-permute-done.18.from_back, ...), custom_call_target="tpu_custom_call" | custom-call | flops 20000000 | bytes 5455872 | tf_op jit(solution)/shard_map/pallas_call | solution.py:84
  133.9 8.5 %collective-permute-start.20 = (f32[896,128]{1,0:T(8,128)S(1)}, f32[896,128]{1,0:T(8,128)S(1)}, u32[]{:S(2)}, u32[]{:S(2)}) collective-permute-start(f32[896,128]{1,0:T(8,128)S(1)} %get-tuple-element.78), channel_id=1, source_target_pairs={{0,1},{1,4},{4,5},{5,8},{8,9},{9,12},{12,13},{13,14},{14,15},{15,1... | collective-permute-start | bytes 1376264 | tf_op jit(solution)/shard_map/ppermute | solution.py:540
  144.0 2.2 %collective-permute-done.21.from_on = f32[896,128]{1,0:T(8,128)S(1)} collective-permute-done((f32[896,128]{1,0:T(8,128)S(1)}, f32[896,128]{1,0:T(8,128)S(1)}, u32[]{:S(2)}, u32[]{:S(2)}) %collective-permute-start.21) | collective-permute-done | bytes 458784 | tf_op jit(solution)/shard_map/ppermute | solution.py:541
  146.2 10.5 %shard_map.122 = (f32[176,128]{1,0:T(8,128)S(1)}, f32[176,128]{1,0:T(8,128)S(1)}, f32[176,128]{1,0:T(8,128)S(1)}, f32[176,128]{1,0:T(8,128)S(1)}) custom-call(s32[2]{0:T(128)S(1)} %pad_add_fusion.ints, f32[1024,128]{1,0:T(8,128)S(1)} %get-tuple-element.77.state, f32[896,128]{1,0:T(8,128)S(1)} %collective-permute-done.20.from_back, ...), custom_call_target="tpu_custom_call" | custom-call | flops 20000000 | bytes 4112384 | tf_op jit(solution)/shard_map/pallas_call | solution.py:84
  157.4 9.8 %collective-permute-start.23 = (f32[176,128]{1,0:T(8,128)S(1)}, f32[176,128]{1,0:T(8,128)S(1)}, u32[]{:S(2)}, u32[]{:S(2)}) collective-permute-start(f32[176,128]{1,0:T(8,128)S(1)} %get-tuple-element.83), channel_id=1, source_target_pairs={{1,0},{9,1},{15,2},{7,3},{0,4},{8,5},{14,6},{6,7},{5,8},{13,9},{11... | collective-permute-start | bytes 270344 | tf_op jit(solution)/shard_map/ppermute | solution.py:642
  167.2 4.7 %collective-permute-start.24 = (f32[176,128]{1,0:T(8,128)S(1)}, f32[176,128]{1,0:T(8,128)S(1)}, u32[]{:S(2)}, u32[]{:S(2)}) collective-permute-start(f32[176,128]{1,0:T(8,128)S(1)} %get-tuple-element.84), channel_id=1, source_target_pairs={{4,0},{12,1},{10,2},{2,3},{5,4},{13,5},{11,6},{3,7},{0,8},{8,9},{1... | collective-permute-start | bytes 270344 | tf_op jit(solution)/shard_map/ppermute | solution.py:642
  175.1 2.7 %collective-permute-done.25.refs_3_ = f32[176,128]{1,0:T(8,128)S(1)} collective-permute-done((f32[176,128]{1,0:T(8,128)S(1)}, f32[176,128]{1,0:T(8,128)S(1)}, u32[]{:S(2)}, u32[]{:S(2)}) %collective-permute-start.25) | collective-permute-done | bytes 90144 | tf_op jit(solution)/shard_map/ppermute | solution.py:642
  (64 shorter events, 23.1 us)
Async XLA Ops:
  5.2 9.4 %collective-permute-start.6 = (f32[392,128]{1,0:T(8,128)S(1)}, f32[392,128]{1,0:T(8,128)S(1)}, u32[]{:S(2)}, u32[]{:S(2)}) collective-permute-start(f32[392,128]{1,0:T(8,128)S(1)} %get-tuple-element.52), channel_id=1, source_target_pairs={{0,0},{1,8},{2,14},{3,6},{4,1},{5,9},{6,15},{7,7},{8,4},{9,12},{10... | collective-permute-start | bytes 602120 | tf_op jit(solution)/shard_map/ppermute | solution.py:551
  5.9 10.1 %collective-permute-start.7 = (f32[392,128]{1,0:T(8,128)S(1)}, f32[392,128]{1,0:T(8,128)S(1)}, u32[]{:S(2)}, u32[]{:S(2)}) collective-permute-start(f32[392,128]{1,0:T(8,128)S(1)} %get-tuple-element.53), channel_id=1, source_target_pairs={{0,1},{1,9},{2,15},{3,7},{4,0},{5,8},{6,14},{7,6},{8,5},{9,13},{10... | collective-permute-start | bytes 602120 | tf_op jit(solution)/shard_map/ppermute | solution.py:551
  11.3 16.8 %collective-permute-start.8 = (f32[392,128]{1,0:T(8,128)S(1)}, f32[392,128]{1,0:T(8,128)S(1)}, u32[]{:S(2)}, u32[]{:S(2)}) collective-permute-start(f32[392,128]{1,0:T(8,128)S(1)} %get-tuple-element.54), channel_id=1, source_target_pairs={{0,4},{1,12},{2,10},{3,2},{4,5},{5,13},{6,11},{7,3},{8,0},{9,8},{1... | collective-permute-start | bytes 602120 | tf_op jit(solution)/shard_map/ppermute | solution.py:551
  11.3 16.8 %collective-permute-start.9 = (f32[392,128]{1,0:T(8,128)S(1)}, f32[392,128]{1,0:T(8,128)S(1)}, u32[]{:S(2)}, u32[]{:S(2)}) collective-permute-start(f32[392,128]{1,0:T(8,128)S(1)} %get-tuple-element.55), channel_id=1, source_target_pairs={{0,5},{1,13},{2,11},{3,3},{4,4},{5,12},{6,10},{7,2},{8,1},{9,9},{1... | collective-permute-start | bytes 602120 | tf_op jit(solution)/shard_map/ppermute | solution.py:551
  28.4 5.6 %collective-permute-start.10 = (f32[1280,128]{1,0:T(8,128)S(1)}, f32[1280,128]{1,0:T(8,128)S(1)}, u32[]{:S(2)}, u32[]{:S(2)}) collective-permute-start(f32[1280,128]{1,0:T(8,128)S(1)} %get-tuple-element.57), channel_id=1, source_target_pairs={{0,1},{1,4},{4,5},{5,8},{8,9},{9,12},{12,13},{13,14},{14,15},{15,1... | collective-permute-start | bytes 1966088 | tf_op jit(solution)/shard_map/ppermute | solution.py:540
  45.7 16.3 %collective-permute-start.12 = (f32[896,128]{1,0:T(8,128)S(1)}, f32[896,128]{1,0:T(8,128)S(1)}, u32[]{:S(2)}, u32[]{:S(2)}) collective-permute-start(f32[896,128]{1,0:T(8,128)S(1)} %get-tuple-element.63), channel_id=1, source_target_pairs={{0,1},{1,4},{4,5},{5,8},{8,9},{9,12},{12,13},{13,14},{14,15},{15,1... | collective-permute-start | bytes 1376264 | tf_op jit(solution)/shard_map/ppermute | solution.py:540
  55.5 9.7 %collective-permute-start.13 = (f32[896,128]{1,0:T(8,128)S(1)}, f32[896,128]{1,0:T(8,128)S(1)}, u32[]{:S(2)}, u32[]{:S(2)}) collective-permute-start(f32[896,128]{1,0:T(8,128)S(1)} %get-tuple-element.64), channel_id=1, source_target_pairs={{1,0},{4,1},{5,4},{8,5},{9,8},{12,9},{13,12},{14,13},{15,14},{10,1... | collective-permute-start | bytes 1376264 | tf_op jit(solution)/shard_map/ppermute | solution.py:541
  57.1 20.6 %collective-permute-start = (f32[304,128]{1,0:T(8,128)S(1)}, f32[304,128]{1,0:T(8,128)S(1)}, u32[]{:S(2)}, u32[]{:S(2)}) collective-permute-start(f32[304,128]{1,0:T(8,128)S(1)} %get-tuple-element.45), channel_id=1, source_target_pairs={{0,0},{1,8},{2,14},{3,6},{4,1},{5,9},{6,15},{7,7},{8,4},{9,12},{10... | collective-permute-start | bytes 466952 | tf_op jit(solution)/shard_map/ppermute | solution.py:570
  57.8 21.2 %collective-permute-start.1 = (f32[304,128]{1,0:T(8,128)S(1)}, f32[304,128]{1,0:T(8,128)S(1)}, u32[]{:S(2)}, u32[]{:S(2)}) collective-permute-start(f32[304,128]{1,0:T(8,128)S(1)} %get-tuple-element.46), channel_id=1, source_target_pairs={{0,1},{1,9},{2,15},{3,7},{4,0},{5,8},{6,14},{7,6},{8,5},{9,13},{10... | collective-permute-start | bytes 466952 | tf_op jit(solution)/shard_map/ppermute | solution.py:570
  61.9 17.1 %collective-permute-start.2 = (f32[304,128]{1,0:T(8,128)S(1)}, f32[304,128]{1,0:T(8,128)S(1)}, u32[]{:S(2)}, u32[]{:S(2)}) collective-permute-start(f32[304,128]{1,0:T(8,128)S(1)} %get-tuple-element.47), channel_id=1, source_target_pairs={{0,4},{1,12},{2,10},{3,2},{4,5},{5,13},{6,11},{7,3},{8,0},{9,8},{1... | collective-permute-start | bytes 466952 | tf_op jit(solution)/shard_map/ppermute | solution.py:570
  62.0 17.1 %collective-permute-start.3 = (f32[304,128]{1,0:T(8,128)S(1)}, f32[304,128]{1,0:T(8,128)S(1)}, u32[]{:S(2)}, u32[]{:S(2)}) collective-permute-start(f32[304,128]{1,0:T(8,128)S(1)} %get-tuple-element.48), channel_id=1, source_target_pairs={{0,5},{1,13},{2,11},{3,3},{4,4},{5,12},{6,10},{7,2},{8,1},{9,9},{1... | collective-permute-start | bytes 466952 | tf_op jit(solution)/shard_map/ppermute | solution.py:570
  74.5 9.1 %collective-permute-start.14 = (f32[896,128]{1,0:T(8,128)S(1)}, f32[896,128]{1,0:T(8,128)S(1)}, u32[]{:S(2)}, u32[]{:S(2)}) collective-permute-start(f32[896,128]{1,0:T(8,128)S(1)} %get-tuple-element.66), channel_id=1, source_target_pairs={{0,1},{1,4},{4,5},{5,8},{8,9},{9,12},{12,13},{13,14},{14,15},{15,1... | collective-permute-start | bytes 1376264 | tf_op jit(solution)/shard_map/ppermute | solution.py:540
  77.7 5.9 %collective-permute-start.15 = (f32[896,128]{1,0:T(8,128)S(1)}, f32[896,128]{1,0:T(8,128)S(1)}, u32[]{:S(2)}, u32[]{:S(2)}) collective-permute-start(f32[896,128]{1,0:T(8,128)S(1)} %get-tuple-element.67), channel_id=1, source_target_pairs={{1,0},{4,1},{5,4},{8,5},{9,8},{12,9},{13,12},{14,13},{15,14},{10,1... | collective-permute-start | bytes 1376264 | tf_op jit(solution)/shard_map/ppermute | solution.py:541
  79.2 22.8 %collective-permute-start.4 = (f32[896,128]{1,0:T(8,128)S(1)}, f32[896,128]{1,0:T(8,128)S(1)}, u32[]{:S(2)}, u32[]{:S(2)}) collective-permute-start(f32[896,128]{1,0:T(8,128)S(1)} %get-tuple-element.50), channel_id=1, source_target_pairs={{0,1},{1,4},{4,5},{5,8},{8,9},{9,12},{12,13},{13,14},{14,15},{15,1... | collective-permute-start | bytes 1376264 | tf_op jit(solution)/shard_map/ppermute | solution.py:540
  82.3 19.7 %collective-permute-start.5 = (f32[896,128]{1,0:T(8,128)S(1)}, f32[896,128]{1,0:T(8,128)S(1)}, u32[]{:S(2)}, u32[]{:S(2)}) collective-permute-start(f32[896,128]{1,0:T(8,128)S(1)} %get-tuple-element.51), channel_id=1, source_target_pairs={{1,0},{4,1},{5,4},{8,5},{9,8},{12,9},{13,12},{14,13},{15,14},{10,1... | collective-permute-start | bytes 1376264 | tf_op jit(solution)/shard_map/ppermute | solution.py:541
  92.9 9.2 %collective-permute-start.17 = (f32[56,512]{1,0:T(8,128)S(1)}, f32[56,512]{1,0:T(8,128)S(1)}, u32[]{:S(2)}, u32[]{:S(2)}) collective-permute-start(f32[56,512]{1,0:T(8,128)S(1)} %get-tuple-element.71.misfit), channel_id=1, source_target_pairs={{1,0},{4,1},{5,4},{8,5},{9,8},{12,9},{13,12},{14,13},{15,14},{10,1... | collective-permute-start | bytes 344072 | tf_op jit(solution)/shard_map/ppermute | solution.py:541
  94.2 8.5 %collective-permute-start.16 = (f32[56,512]{1,0:T(8,128)S(1)}, f32[56,512]{1,0:T(8,128)S(1)}, u32[]{:S(2)}, u32[]{:S(2)}) collective-permute-start(f32[56,512]{1,0:T(8,128)S(1)} %get-tuple-element.71.misfit), channel_id=1, source_target_pairs={{0,1},{1,4},{4,5},{5,8},{8,9},{9,12},{12,13},{13,14},{14,15},{15,1... | collective-permute-start | bytes 344072 | tf_op jit(solution)/shard_map/ppermute | solution.py:540
  113.3 5.9 %collective-permute-start.18 = (f32[896,128]{1,0:T(8,128)S(1)}, f32[896,128]{1,0:T(8,128)S(1)}, u32[]{:S(2)}, u32[]{:S(2)}) collective-permute-start(f32[896,128]{1,0:T(8,128)S(1)} %get-tuple-element.73), channel_id=1, source_target_pairs={{0,1},{1,4},{4,5},{5,8},{8,9},{9,12},{12,13},{13,14},{14,15},{15,1... | collective-permute-start | bytes 1376264 | tf_op jit(solution)/shard_map/ppermute | solution.py:540
  117.8 5.6 %collective-permute-start.19 = (f32[896,128]{1,0:T(8,128)S(1)}, f32[896,128]{1,0:T(8,128)S(1)}, u32[]{:S(2)}, u32[]{:S(2)}) collective-permute-start(f32[896,128]{1,0:T(8,128)S(1)} %get-tuple-element.74), channel_id=1, source_target_pairs={{1,0},{4,1},{5,4},{8,5},{9,8},{12,9},{13,12},{14,13},{15,14},{10,1... | collective-permute-start | bytes 1376264 | tf_op jit(solution)/shard_map/ppermute | solution.py:541
  133.9 10.0 %collective-permute-start.20 = (f32[896,128]{1,0:T(8,128)S(1)}, f32[896,128]{1,0:T(8,128)S(1)}, u32[]{:S(2)}, u32[]{:S(2)}) collective-permute-start(f32[896,128]{1,0:T(8,128)S(1)} %get-tuple-element.78), channel_id=1, source_target_pairs={{0,1},{1,4},{4,5},{5,8},{8,9},{9,12},{12,13},{13,14},{14,15},{15,1... | collective-permute-start | bytes 1376264 | tf_op jit(solution)/shard_map/ppermute | solution.py:540
  156.7 17.3 %collective-permute-start.22 = (f32[176,128]{1,0:T(8,128)S(1)}, f32[176,128]{1,0:T(8,128)S(1)}, u32[]{:S(2)}, u32[]{:S(2)}) collective-permute-start(f32[176,128]{1,0:T(8,128)S(1)} %get-tuple-element.82), channel_id=1, source_target_pairs={{0,0},{8,1},{14,2},{6,3},{1,4},{9,5},{15,6},{7,7},{4,8},{12,9},{10... | collective-permute-start | bytes 270344 | tf_op jit(solution)/shard_map/ppermute | solution.py:642
  157.4 16.6 %collective-permute-start.23 = (f32[176,128]{1,0:T(8,128)S(1)}, f32[176,128]{1,0:T(8,128)S(1)}, u32[]{:S(2)}, u32[]{:S(2)}) collective-permute-start(f32[176,128]{1,0:T(8,128)S(1)} %get-tuple-element.83), channel_id=1, source_target_pairs={{1,0},{9,1},{15,2},{7,3},{0,4},{8,5},{14,6},{6,7},{5,8},{13,9},{11... | collective-permute-start | bytes 270344 | tf_op jit(solution)/shard_map/ppermute | solution.py:642
  167.2 7.9 %collective-permute-start.24 = (f32[176,128]{1,0:T(8,128)S(1)}, f32[176,128]{1,0:T(8,128)S(1)}, u32[]{:S(2)}, u32[]{:S(2)}) collective-permute-start(f32[176,128]{1,0:T(8,128)S(1)} %get-tuple-element.84), channel_id=1, source_target_pairs={{4,0},{12,1},{10,2},{2,3},{5,4},{13,5},{11,6},{3,7},{0,8},{8,9},{1... | collective-permute-start | bytes 270344 | tf_op jit(solution)/shard_map/ppermute | solution.py:642
  171.8 6.0 %collective-permute-start.25 = (f32[176,128]{1,0:T(8,128)S(1)}, f32[176,128]{1,0:T(8,128)S(1)}, u32[]{:S(2)}, u32[]{:S(2)}) collective-permute-start(f32[176,128]{1,0:T(8,128)S(1)} %get-tuple-element.85), channel_id=1, source_target_pairs={{5,0},{13,1},{11,2},{3,3},{4,4},{12,5},{10,6},{2,7},{1,8},{9,9},{1... | collective-permute-start | bytes 270344 | tf_op jit(solution)/shard_map/ppermute | solution.py:642
  (12 other events, 81.3 us)

commit v2 on v0

--- a/solution.py
+++ b/solution.py
@@ -1,14 +1,775 @@
+import functools
+
 import jax
 import jax.numpy as jnp
 from jax import lax
+from jax.experimental import pallas as pl
+from jax.experimental.pallas import tpu as pltpu
 from jax.sharding import PartitionSpec as P
 
 STEPS = 12
 SPONGE = 8
+REACH = 4
+DEPTH = 4
+LANES = 128
+ROWS = 8
 
 
 stencil = (-205.0 / 72.0, 8.0 / 5.0, -1.0 / 5.0, 8.0 / 315.0, -1.0 / 560.0)
 damping_peak = 0.3
+
+
+class Layout:
+    def __init__(self, count_x, count_y, width_x, width_y):
+        self.count_x, self.count_y = count_x, count_y
+        self.width_x, self.width_y = width_x, width_y
+        self.chunk = width_y // count_x
+        self.wide = width_x * count_x
+        self.tiles = self.wide // ROWS
+        self.whole_y = width_y * count_y
+        self.margin = REACH * DEPTH
+        self.extent = self.chunk + 2 * self.margin
+        self.stride = self.tiles * 2 * ROWS
+        self.padded_rows = self.extent * self.stride + ROWS
+        self.kept = self.margin - REACH
+        self.inner = self.extent - 2 * REACH
+        self.rows = self.chunk * self.wide
+        self.cells = self.chunk * width_x
+        self.near = self.chunk + 2 * REACH
+        self.state_rows = (self.chunk + self.near) * self.wide
+        self.lacking = range(REACH, self.chunk - REACH)
+        self.send_rows = (self.chunk + len(self.lacking)) * self.wide
+
+    def at(self, place):
+        pair, rest = divmod(place, 2 * self.count_x)
+        chip, core = divmod(rest, 2)
+        slab = chip if pair % 2 == 0 else self.count_x - 1 - chip
+        return slab * self.count_y + 2 * pair + core
+
+    def to_chunks(self, turn):
+        moves = []
+        for slab in range(self.count_x):
+            for strip in range(self.count_y):
+                moves.append((slab * self.count_y + strip, self.at(strip * self.count_x + (slab ^ turn))))
+        return moves
+
+    def to_slabs(self, turn):
+        return [(target, source) for source, target in self.to_chunks(turn)]
+
+    def swaps(self, first):
+        moves = []
+        for place in range(first, self.count_x * self.count_y - 1, 2):
+            moves += [(self.at(place), self.at(place + 1)), (self.at(place + 1), self.at(place))]
+        return moves
+
+
+def fits(count_x, count_y, width_x, width_y, depth_z):
+    return (
+        count_x & (count_x - 1) == 0
+        and count_y % 2 == 0
+        and width_x == ROWS
+        and width_x * count_x == ROWS * REACH
+        and depth_z == LANES
+        and width_y == count_x * REACH * DEPTH
+    )
+
+
+def f32(*shape):
+    return jax.ShapeDtypeStruct(shape, jnp.float32)
+
+
+def call(kernel, ints, arrays, outs, scratch=(), cost=1_000_000, space=pltpu.VMEM, aliases=None):
+    return pl.pallas_call(
+        kernel,
+        out_shape=tuple(outs),
+        in_specs=[pl.BlockSpec(memory_space=pltpu.SMEM)] * len(ints)
+        + [pl.BlockSpec(memory_space=space)] * len(arrays),
+        out_specs=tuple(pl.BlockSpec(memory_space=pltpu.VMEM) for _ in outs),
+        scratch_shapes=list(scratch),
+        input_output_aliases=aliases or {},
+        compiler_params=pltpu.CompilerParams(vmem_limit_bytes=32 * 1024 * 1024),
+        cost_estimate=pl.CostEstimate(flops=cost, bytes_accessed=cost, transcendentals=0),
+    )(*ints, *arrays)
+
+
+def aligned(value, to=ROWS):
+    return pl.multiple_of(value, to)
+
+
+def cut_fields(lay, slab, fields, fill, targets):
+    for turn, target in enumerate(targets):
+        start = (slab ^ turn) * lay.chunk
+        row = 0
+        for field in fields:
+            for y in range(lay.chunk):
+                target[row : row + ROWS, :] = field[pl.ds(start + y, ROWS, stride=lay.width_y), :]
+                row += ROWS
+        fill(target, row)
+
+
+def cut_forward(lay, slab_ref, count_ref, now, prev, courant, cell, *refs):
+    sends, (held, held_cell, done) = refs[: lay.count_x], refs[lay.count_x :]
+    copies = []
+    for index, (source, target) in enumerate(
+        [(cell, held_cell)] + [(field, held.at[place]) for place, field in enumerate((now, prev, courant))]
+    ):
+        copies.append(pltpu.make_async_copy(source, target, done.at[index]))
+        copies[-1].start()
+    for copy in copies:
+        copy.wait()
+    slots = lax.broadcasted_iota(jnp.int32, (1, LANES), 1)
+
+    def fill(target, row):
+        for tile in range(lay.count_x):
+            used = jnp.where(slots < count_ref[tile], held_cell[tile : tile + 1, :], -1)
+            target[row + tile : row + tile + 1, :] = used.astype(jnp.float32)
+
+    cut_fields(lay, slab_ref[0], [held.at[place] for place in range(3)], fill, sends)
+
+
+def cut_adjoint(lay, slab_ref, now, prev, observed, *sends):
+    def fill(target, row):
+        target[row : row + observed.shape[0], :] = observed[...]
+
+    cut_fields(lay, slab_ref[0], (now, prev), fill, sends)
+
+
+def join_fields(lay, own_slot, odd, pieces, joined, state, courant, send_next, send_twin):
+    fields = joined.shape[0]
+    for turn, piece in enumerate(pieces):
+        start_x = (own_slot ^ turn) * ROWS
+        for field in range(fields):
+            for y in range(lay.chunk):
+                row = (field * lay.chunk + y) * ROWS
+                joined[field, pl.ds(aligned(y * lay.wide + start_x), ROWS), :] = piece[row : row + ROWS, :]
+    kept_rows = lay.kept * lay.wide
+    for field in range(fields):
+        target, first = (state, 0) if field == 0 else (state, (lay.chunk + REACH) * lay.wide)
+        if field == 2:
+            target, first = courant, 0
+        for y in range(lay.chunk):
+            for tile in range(lay.tiles):
+                values = joined[field, pl.ds(y * lay.wide + tile, ROWS, stride=lay.tiles), :]
+                row = y * lay.wide + tile * ROWS
+                target[first + row : first + row + ROWS, :] = values
+                if field == 0:
+                    send_next[row : row + ROWS, :] = values
+                    send_twin[row : row + ROWS, :] = values
+    for field in range(1, fields):
+        source, first = (state, (lay.chunk + REACH) * lay.wide) if field == 1 else (courant, 0)
+        place = lay.rows + (field - 1) * kept_rows
+        skipped = (lay.chunk - lay.kept) * lay.wide
+        ahead = source[pl.ds(aligned(first + odd * skipped), kept_rows), :]
+        send_next[place : place + kept_rows, :] = ahead
+        behind = source[pl.ds(aligned(first + (1 - odd) * skipped), kept_rows), :]
+        send_twin[place : place + kept_rows, :] = behind
+
+
+def join_forward(lay, where_ref, *refs):
+    pieces, (state, courant, send_next, send_twin, codes, joined) = refs[: lay.count_x], refs[lay.count_x :]
+    own_slot, odd = where_ref[0], where_ref[1]
+    join_fields(lay, own_slot, odd, pieces, joined, state, courant, send_next, send_twin)
+    first = 3 * lay.cells
+    strip_cells = lay.width_y * LANES
+    slab_row = lax.broadcasted_iota(jnp.int32, codes.shape, 0)
+    found = jnp.full(codes.shape, -1.0, jnp.float32)
+    for turn, piece in enumerate(pieces):
+        cell = piece[first : first + lay.count_x, :].astype(jnp.int32)
+        used = cell >= 0
+        cell = jnp.maximum(cell, 0)
+        x = lax.div(cell, jnp.int32(strip_cells))
+        y = lax.rem(lax.div(cell, jnp.int32(LANES)), jnp.int32(lay.width_y)) - own_slot * lay.chunk
+        inside = used & (y >= 0) & (y < lay.chunk)
+        code = jnp.where(inside, (y * ROWS + x) * LANES + lax.rem(cell, jnp.int32(LANES)), -1)
+        code = code.astype(jnp.float32)
+        line = jnp.concatenate([code[tile : tile + 1, :] for tile in range(lay.count_x)], axis=1)
+        found = jnp.where(slab_row == (own_slot ^ turn), jnp.broadcast_to(line, codes.shape), found)
+    codes[...] = found
+
+
+def join_adjoint(lay, where_ref, *refs):
+    pieces, (state, send_next, send_twin, joined) = refs[: lay.count_x], refs[lay.count_x :]
+    join_fields(lay, where_ref[0], where_ref[1], pieces, joined, state, None, send_next, send_twin)
+
+
+def load_state(lay, odd, first, now, prev, state, from_next, from_twin):
+    zeros = jnp.zeros((ROWS, LANES), jnp.float32)
+    for row in range(0, lay.padded_rows, 2 * ROWS):
+        now[row : row + ROWS, :] = zeros
+        prev[row : row + ROWS, :] = zeros
+
+    def put(buffer, layer, ref, source):
+        for tile in range(lay.tiles):
+            row = layer * lay.stride + (2 * tile + 1) * ROWS
+            values = ref[source * lay.wide + tile * ROWS : source * lay.wide + (tile + 1) * ROWS, :]
+            buffer[pl.ds(row if isinstance(row, int) else aligned(row), ROWS), :] = values
+
+    ahead = lay.margin + lay.chunk
+    for y in range(lay.chunk):
+        put(now, lay.margin + y, state, y)
+        put(now, odd * ahead + y, from_next, y)
+        put(now, (1 - odd) * ahead + y, from_twin, y)
+    if first:
+        for y in range(lay.chunk):
+            put(prev, lay.margin + y, state, lay.chunk + REACH + y)
+        for y in range(lay.kept):
+            put(prev, odd * ahead + (1 - odd) * REACH + y, from_next, lay.chunk + y)
+            put(prev, (1 - odd) * ahead + odd * REACH + y, from_twin, lay.chunk + y)
+        return
+    for y in range(lay.near):
+        put(prev, lay.margin - REACH + y, state, lay.chunk + y)
+    for index, y in enumerate(lay.lacking):
+        put(prev, odd * ahead + y, from_next, lay.chunk + index)
+        put(prev, (1 - odd) * ahead + y, from_twin, lay.chunk + index)
+
+
+def store_state(lay, now, prev, state, send):
+    def put(refs, target, buffer, layer):
+        for tile in range(lay.tiles):
+            row = layer * lay.stride + (2 * tile + 1) * ROWS
+            values = buffer[row : row + ROWS, :]
+            for ref, place in refs:
+                ref[place * lay.wide + tile * ROWS : place * lay.wide + (tile + 1) * ROWS, :] = values
+
+    for y in range(lay.chunk):
+        put([(state, y), (send, y)], y, now, lay.margin + y)
+    for y in range(lay.near):
+        refs = [(state, lay.chunk + y)]
+        if y - REACH in lay.lacking:
+            refs.append((send, lay.chunk + y - REACH - lay.lacking[0]))
+        put(refs, y, prev, lay.margin - REACH + y)
+
+
+def split(values):
+    high = values.astype(jnp.bfloat16)
+    rest = values - high.astype(jnp.float32)
+    middle = rest.astype(jnp.bfloat16)
+    low = (rest - middle.astype(jnp.float32)).astype(jnp.bfloat16)
+    return high, middle, low
+
+
+def fill_band(band):
+    apart = lax.broadcasted_iota(jnp.int32, (LANES, LANES), 0) - lax.broadcasted_iota(
+        jnp.int32, (LANES, LANES), 1
+    )
+    weights = jnp.where(apart == 0, 3.0 * stencil[0], 0.0).astype(jnp.float32)
+    for k in range(1, REACH + 1):
+        weights = jnp.where(jnp.abs(apart) == k, stencil[k], weights)
+    high, middle, low = split(weights)
+    for index, part in enumerate((high, high, high, middle, middle, low)):
+        band[index * LANES : (index + 1) * LANES, :] = part
+
+
+def sweep(lay, step, now, prev, following, half, gain, band, inject=None):
+    first_layer = REACH * (step + 1)
+    group = 8
+
+    def layers(block, carry):
+        start = first_layer + group * block
+
+        def rows_of(y, tile, shift=0):
+            return pl.ds(aligned(y * lay.stride + (2 * tile + 1) * ROWS) + shift, ROWS)
+
+        centers = [
+            [now[rows_of(start + inner, tile), :] for tile in range(lay.tiles)] for inner in range(group)
+        ]
+        stacked = jnp.concatenate([tile for layer in centers for tile in layer], axis=0)
+        high, middle, low = split(stacked)
+        along_z = jnp.dot(
+            jnp.concatenate([high, middle, low, high, middle, high], axis=1),
+            band[...],
+            preferred_element_type=jnp.float32,
+        )
+        for inner in range(group):
+            y = start + inner
+            lower = [now[rows_of(y, tile, -1), :] for tile in range(lay.tiles)]
+            upper = [now[rows_of(y, tile, 1), :] for tile in range(lay.tiles)]
+
+            def at_x(tile):
+                if tile < 0:
+                    return lower[tile + lay.tiles]
+                if tile >= lay.tiles:
+                    return upper[tile - lay.tiles]
+                return centers[inner][tile]
+
+            for tile in range(lay.tiles):
+                place = (inner * lay.tiles + tile) * ROWS
+                total = along_z[place : place + ROWS, :]
+                for k in range(1, REACH + 1):
+                    pair = now[rows_of(y + k, tile), :] + now[rows_of(y - k, tile), :]
+                    total = total + stencil[k] * (pair + (at_x(tile - k) + at_x(tile + k)))
+                flat = aligned((y - REACH) * lay.wide + tile * ROWS)
+                if inject is not None:
+                    spread_rows = pl.ds((y - REACH) * lay.wide + tile, ROWS, stride=lay.tiles)
+                    total = total + inject[step, spread_rows, :]
+                former = prev[rows_of(y, tile), :]
+                change = (centers[inner][tile] - former) + half[pl.ds(flat, ROWS), :] * total
+                following[rows_of(y, tile), :] = former + gain[pl.ds(flat, ROWS), :] * change
+        return carry
+
+    lax.fori_loop(0, (lay.extent - 2 * first_layer) // group, layers, 0)
+
+
+def zero_between(lay, buffer):
+    zeros = jnp.zeros((ROWS, LANES), jnp.float32)
+    for row in range(0, lay.padded_rows, 2 * ROWS):
+        buffer[row : row + ROWS, :] = zeros
+
+
+def keep_own(lay, step, following, history):
+    for y in range(lay.chunk):
+        for tile in range(lay.tiles):
+            row = (lay.margin + y) * lay.stride + (2 * tile + 1) * ROWS
+            place = step * lay.rows + y * lay.wide + tile * ROWS
+            history[place : place + ROWS, :] = following[row : row + ROWS, :]
+
+
+def forward(lay, phase, sources, ints, state, from_next, from_twin, courant, gain, drive, *refs):
+    first, last = phase == 0, phase == STEPS // DEPTH - 1
+    refs = list(refs)
+    history = refs.pop(0)
+    half = refs.pop(0) if first else courant
+    if not last:
+        state_out, send = refs.pop(0), refs.pop(0)
+    now, prev, following, band, pulse = refs
+    odd = ints[0]
+
+    fill_band(band)
+    load_state(lay, odd, first, now, prev, state, from_next, from_twin)
+    zero_between(lay, following)
+    if first:
+        tail = (lay.chunk + lay.kept) * lay.wide
+        part = lay.kept * lay.wide
+        half[part : part + lay.rows, :] = 0.5 * courant[...]
+        ahead = part + lay.rows
+        half[pl.ds(aligned(odd * ahead), part), :] = 0.5 * from_next[tail : tail + part, :]
+        half[pl.ds(aligned((1 - odd) * ahead), part), :] = 0.5 * from_twin[tail : tail + part, :]
+    for source in range(sources):
+        flat = pl.ds(ints[1 + sources + source], 1)
+        pulse[source : source + 1, :] = half[flat, :] * gain[flat, :]
+
+    for step in range(DEPTH):
+        sweep(lay, step, now, prev, following, half, gain, band)
+        added = pulse[...] * drive[phase * DEPTH + step]
+        places = [pl.ds(ints[1 + source], 1) for source in range(sources)]
+        lines = [following[place, :] for place in places]
+        for source, (place, line) in enumerate(zip(places, lines)):
+            following[place, :] = line + added[source : source + 1, :]
+        keep_own(lay, step, following, history)
+        now, prev, following = following, now, prev
+
+    if not last:
+        store_state(lay, now, prev, state_out, send)
+
+
+def slot_rows(codes, slab):
+    code = codes[slab : slab + 1, :].astype(jnp.int32)
+    row = jnp.where(code >= 0, lax.shift_right_arithmetic(code, 7), -1)
+    return row, jnp.where(code >= 0, code & (LANES - 1), -1)
+
+
+def record_slots(lay, history, codes, plain, stash, record):
+    for step in range(DEPTH):
+        for y in range(lay.chunk):
+            for tile in range(lay.tiles):
+                row = step * lay.rows + y * lay.wide
+                values = history[row + tile * ROWS : row + (tile + 1) * ROWS, :]
+                plain[pl.ds(row + tile, ROWS, stride=lay.tiles), :] = values
+    for slab in range(lay.count_x):
+        for step in range(DEPTH):
+            for y in range(lay.chunk):
+                row = step * lay.rows + y * lay.wide + slab * ROWS
+                target = ((slab * DEPTH + step) * lay.chunk + y) * ROWS
+                stash[target : target + ROWS, :] = plain[row : row + ROWS, :]
+    slots = codes.shape[1]
+    width = 2 * LANES
+    for slab in range(lay.count_x):
+        cell_row, cell_z = slot_rows(codes, slab)
+        parts = split(stash[slab * DEPTH * lay.cells : (slab + 1) * DEPTH * lay.cells, :])
+        parts = jnp.concatenate(parts, axis=1)
+        for start in range(0, slots, width):
+            here = slice(start, start + width)
+            z = lax.broadcasted_iota(jnp.int32, (LANES, width), 0)
+            pick = jnp.where(z == cell_z[:, here], 1.0, 0.0).astype(jnp.bfloat16)
+            found = jnp.dot(parts, jnp.concatenate([pick] * 3, axis=0), preferred_element_type=jnp.float32)
+            wanted = lax.broadcasted_iota(jnp.int32, (lay.cells, width), 0) == cell_row[:, here]
+            for step in range(DEPTH):
+                part = jnp.where(wanted, found[step * lay.cells : (step + 1) * lay.cells, :], 0.0)
+                row = step * lay.count_x + slab
+                record[row : row + 1, here] = jnp.sum(part, axis=0, keepdims=True)
+
+
+def record_phase(lay, history, codes, record, plain, stash):
+    record_slots(lay, history, codes, plain, stash, record)
+
+
+def record_last(lay, phases, where_ref, history, codes, *refs):
+    earlier, refs = refs[: phases - 1], refs[phases - 1 :]
+    observed, (misfit, plain, stash, record) = refs[: lay.count_x], refs[lay.count_x :]
+    record_slots(lay, history, codes, plain, stash, record)
+    block = DEPTH * lay.count_x
+    for index, part in enumerate(list(earlier) + [record]):
+        misfit[index * block : (index + 1) * block, :] = part[...]
+    total = STEPS * lay.count_x
+    for slab in range(lay.count_x):
+        misfit[total + slab : total + slab + 1, :] = codes[slab : slab + 1, :]
+    for turn, piece in enumerate(observed):
+        place = pl.ds(aligned((where_ref[0] ^ turn) * LANES, LANES), LANES)
+        used = jnp.concatenate([codes[:, place]] * STEPS, axis=0) >= 0
+        seen = piece[2 * lay.cells : 2 * lay.cells + total, :]
+        misfit[0:total, place] = jnp.where(used, misfit[0:total, place] - seen, 0.0)
+
+
+def spread(lay, phase, side, misfit, inject):
+    codes = misfit[STEPS * lay.count_x : (STEPS + 1) * lay.count_x, :]
+    for slab in range(lay.count_x):
+        cell_row, cell_z = slot_rows(codes, slab)
+        slots = cell_row.shape[1]
+        z = lax.broadcasted_iota(jnp.int32, (LANES, slots), 0)
+        pick = jnp.where(z == cell_z, 1.0, 0.0).astype(jnp.bfloat16)
+        hit = lax.broadcasted_iota(jnp.int32, (lay.cells, slots), 0) == cell_row
+        hit = jnp.where(hit, 1.0, 0.0).astype(jnp.bfloat16)
+        left, spans = [], []
+        for step in range(DEPTH):
+            low, high = 0, lay.chunk
+            if side < 0:
+                low = REACH * (step + 1) - lay.margin + lay.chunk
+            if side > 0:
+                high = lay.margin - REACH * (step + 1)
+            if low >= high:
+                continue
+            row = (STEPS - 1 - phase * DEPTH - step) * lay.count_x + slab
+            parts = split(misfit[row : row + 1, :])
+            left.append(jnp.concatenate([hit[low * ROWS : high * ROWS, :] * part for part in parts], axis=1))
+            spans.append((step, low, high))
+        placed = lax.dot_general(
+            jnp.concatenate(left, axis=0),
+            jnp.concatenate([pick] * 3, axis=1),
+            (((1,), (1,)), ((), ())),
+            preferred_element_type=jnp.float32,
+        )
+        at = 0
+        for step, low, high in spans:
+            for y in range(low, high):
+                layer = lay.margin + side * lay.chunk + y - REACH
+                target = layer * lay.wide + slab * ROWS
+                inject[step, target : target + ROWS, :] = placed[at : at + ROWS, :]
+                at += ROWS
+
+
+def spread_own(lay, phase, misfit, inject):
+    spread(lay, phase, 0, misfit, inject)
+
+
+def spread_sides(lay, phase, where_ref, own, misfit_next, misfit_twin, inject):
+    odd = where_ref[1]
+
+    @pl.when(odd == 1)
+    def ahead_is_next():
+        spread(lay, phase, 1, misfit_next, inject)
+        spread(lay, phase, -1, misfit_twin, inject)
+
+    @pl.when(odd == 0)
+    def behind_is_next():
+        spread(lay, phase, -1, misfit_next, inject)
+        spread(lay, phase, 1, misfit_twin, inject)
+
+
+def backward(lay, phase, where_ref, state, from_next, from_twin, half, gain, inject, *refs):
+    first, last = phase == 0, phase == STEPS // DEPTH - 1
+    refs = list(refs)
+    history = refs.pop(0)
+    if not last:
+        state_out, send = refs.pop(0), refs.pop(0)
+    now, prev, following, band = refs
+
+    fill_band(band)
+    load_state(lay, where_ref[1], first, now, prev, state, from_next, from_twin)
+    zero_between(lay, following)
+    for step in range(DEPTH):
+        sweep(lay, step, now, prev, following, half, gain, band, inject)
+        keep_own(lay, step, following, history)
+        now, prev, following = following, now, prev
+    if not last:
+        store_state(lay, now, prev, state_out, send)
+
+
+def add_gradient(lay, before, adjoint, history, state, gradient):
+    def layer(y, carry):
+        place = aligned(y * lay.wide)
+        own = pl.ds(place, lay.wide)
+        fields = [state[pl.ds(aligned(place + (lay.chunk + REACH) * lay.wide), lay.wide), :], state[own, :]]
+        fields += [history[pl.ds(aligned(place + step * lay.rows), lay.wide), :] for step in range(DEPTH)]
+        total = None if before is None else before[own, :]
+        for step in range(DEPTH):
+            index = DEPTH - 1 - step
+            accel = (fields[index + 2] - fields[index + 1]) - (fields[index + 1] - fields[index])
+            term = adjoint[pl.ds(aligned(place + step * lay.rows), lay.wide), :] * accel
+            total = term if total is None else total + term
+        gradient[own, :] = total
+        return carry
+
+    lax.fori_loop(0, lay.chunk, layer, 0)
+
+
+def gradient_first(lay, adjoint, history, state, gradient):
+    add_gradient(lay, None, adjoint, history, state, gradient)
+
+
+def gradient_later(lay, adjoint, history, state, before, gradient):
+    add_gradient(lay, before, adjoint, history, state, gradient)
+
+
+def gradient_last(lay, where_ref, adjoint, history, state, before, misfit, *refs):
+    sends, (gradient, plain) = refs[: lay.count_x], refs[lay.count_x :]
+    add_gradient(lay, before, adjoint, history, state, gradient)
+    for y in range(lay.chunk):
+        for tile in range(lay.tiles):
+            row = y * lay.wide + tile * ROWS
+            plain[pl.ds(y * lay.wide + tile, ROWS, stride=lay.tiles), :] = gradient[row : row + ROWS, :]
+    total = STEPS * lay.count_x
+    for turn, send in enumerate(sends):
+        other = where_ref[0] ^ turn
+        for y in range(lay.chunk):
+            source = pl.ds(aligned(y * lay.wide + other * ROWS), ROWS)
+            send[y * ROWS : (y + 1) * ROWS, :] = plain[source, :]
+        tile = pl.ds(aligned(other * LANES, LANES), LANES)
+        send[lay.cells : lay.cells + total, :] = misfit[0:total, tile]
+
+
+def finish(lay, slab_ref, *refs):
+    pieces, (gradient, residual) = refs[: lay.count_x], refs[lay.count_x :]
+    slab = slab_ref[0]
+    total = None
+    for turn, piece in enumerate(pieces):
+        start = (slab ^ turn) * lay.chunk
+        for x in range(ROWS):
+            target = pl.ds(aligned(x * lay.width_y + start), lay.chunk)
+            gradient[target, :] = piece[pl.ds(x, lay.chunk, stride=ROWS), :]
+        part = piece[lay.cells : lay.cells + residual.shape[0], :]
+        total = part if total is None else total + part
+    residual[...] = total
+
+
+def gain_rows(lay, first_y):
+    x = jnp.arange(ROWS)[None, :] * lay.tiles + jnp.arange(lay.tiles)[:, None]
+    y = first_y + REACH + jnp.arange(lay.inner)
+
+    def ramp(position, count):
+        gap = jnp.minimum(position, count - 1 - position)
+        profile = jnp.maximum(SPONGE - gap, 0).astype(jnp.float32) / SPONGE
+        return profile * profile
+
+    damping = damping_peak * (ramp(x, lay.wide)[None] + ramp(y, lay.whole_y)[:, None, None])
+    gain = (2.0 / (1.0 + damping)).reshape(lay.inner * lay.wide, 1)
+    return jnp.broadcast_to(gain, (lay.inner * lay.wide, LANES))
+
+
+def source_rows(lay, first_y, source_cell, wavelet):
+    x = source_cell // (lay.whole_y * LANES)
+    y = source_cell // LANES % lay.whole_y - first_y
+    z = source_cell % LANES
+    inside = (y >= REACH) & (y < lay.extent - REACH)
+    tile, row = x % lay.tiles, x // lay.tiles
+    padded = jnp.where(inside, y * lay.stride + (2 * tile + 1) * ROWS + row, ROWS // 2)
+    flat = jnp.where(inside, (y - REACH) * lay.wide + tile * ROWS + row, 0)
+    same = (padded[:, None] == padded[None, :]) & inside[None, :]
+    spot = (z[:, None] == jnp.arange(LANES)[None, :]).astype(jnp.float32)
+    lines = jnp.where(same[None, :, :, None], wavelet[:, None, :, None] * spot[None, None], 0.0)
+    return padded, flat, jnp.sum(lines, axis=2)
+
+
+def local_tiles(
+    lay,
+    courant,
+    state_prev,
+    state_now,
+    adjoint_now,
+    adjoint_next,
+    source_cell,
+    wavelet,
+    observed,
+    receiver_cell,
+    receiver_count,
+):
+    axes = ("gx", "gy")
+    slab = lax.axis_index("gx")
+    strip = lax.axis_index("gy")
+    pair = strip // 2
+    chip = jnp.where(pair % 2 == 0, slab, lay.count_x - 1 - slab)
+    place = (pair * lay.count_x + chip) * 2 + strip % 2
+    odd = strip % 2
+    first_y = place * lay.chunk - lay.margin
+    slab_int = slab.reshape(1).astype(jnp.int32)
+    where = jnp.stack([place % lay.count_x, odd]).astype(jnp.int32)
+
+    count = lay.count_x
+    sources = source_cell.shape[0]
+    slots = count * receiver_cell.shape[3]
+    flat = lambda values: values.reshape(-1, LANES)
+    part = functools.partial
+
+    def swap(to_next, to_twin):
+        return (
+            lax.ppermute(to_next, axes, lay.swaps(1)),
+            lax.ppermute(to_twin, axes, lay.swaps(0)),
+        )
+
+    padded, flat_row, drive = source_rows(lay, first_y, source_cell, wavelet)
+    gain = gain_rows(lay, first_y)
+    ints = jnp.concatenate([odd.reshape(1), padded, flat_row]).astype(jnp.int32)
+
+    tail = -(-count // ROWS) * ROWS
+    cuts = call(
+        part(cut_forward, lay),
+        (slab_int, receiver_count.reshape(-1)),
+        (flat(state_now), flat(state_prev), flat(courant), receiver_cell.reshape(count, LANES)),
+        [f32(3 * lay.cells + tail, LANES)] * count,
+        [
+            pltpu.VMEM((3, lay.width_x * lay.width_y, LANES), jnp.float32),
+            pltpu.VMEM((count, LANES), jnp.int32),
+            pltpu.SemaphoreType.DMA((4,)),
+        ],
+        space=pltpu.HBM,
+    )
+    pieces = [lax.ppermute(cut, axes, lay.to_chunks(turn)) for turn, cut in enumerate(cuts)]
+    kept_rows = lay.kept * lay.wide
+    state, own_courant, to_next, to_twin, codes = call(
+        part(join_forward, lay),
+        (where,),
+        pieces,
+        [f32(lay.state_rows, LANES), f32(lay.rows, LANES)]
+        + [f32(lay.rows + 2 * kept_rows, LANES)] * 2
+        + [f32(count, slots)],
+        [pltpu.VMEM((3, lay.rows, LANES), jnp.float32)],
+    )
+    from_next, from_twin = swap(to_next, to_twin)
+
+    traces = flat(observed)
+    cuts = call(
+        part(cut_adjoint, lay),
+        (slab_int,),
+        (flat(adjoint_now), flat(adjoint_next), traces),
+        [f32(2 * lay.cells + traces.shape[0], LANES)] * count,
+    )
+    back_pieces = [lax.ppermute(cut, axes, lay.to_chunks(turn)) for turn, cut in enumerate(cuts)]
+    back_state, to_next, to_twin = call(
+        part(join_adjoint, lay),
+        (where,),
+        back_pieces,
+        [f32(lay.state_rows, LANES)] + [f32(lay.rows + kept_rows, LANES)] * 2,
+        [pltpu.VMEM((2, lay.rows, LANES), jnp.float32)],
+    )
+    back_from_next, back_from_twin = swap(to_next, to_twin)
+
+    phases = STEPS // DEPTH
+    step_cost = 8_000_000
+    side_cost = 4_000_000
+    history_shape = f32(DEPTH * lay.rows, LANES)
+    state_shapes = [f32(lay.state_rows, LANES), f32(lay.send_rows, LANES)]
+    buffers = [pltpu.VMEM((lay.padded_rows, LANES), jnp.float32)] * 3
+    buffers += [pltpu.VMEM((6 * LANES, LANES), jnp.bfloat16)]
+    record_scratch = [pltpu.VMEM((DEPTH * lay.rows, LANES), jnp.float32)] * 2
+    record_shape = (DEPTH * count, slots)
+    histories, states, records = [], [], []
+    half = own_courant
+    for phase in range(phases):
+        first, last = phase == 0, phase == phases - 1
+        outs = [history_shape]
+        if first:
+            outs.append(f32(lay.inner * lay.wide, LANES))
+        if not last:
+            outs += state_shapes
+        results = list(
+            call(
+                part(forward, lay, phase, sources),
+                (ints,),
+                [state, from_next, from_twin, half, gain, drive],
+                outs,
+                buffers + [pltpu.VMEM((sources, LANES), jnp.float32)],
+                cost=step_cost,
+            )
+        )
+        histories.append(results.pop(0))
+        states.append(state)
+        if first:
+            half = results.pop(0)
+        if last:
+            (misfit,) = call(
+                part(record_last, lay, phases),
+                (where,),
+                [histories[-1], codes] + records + back_pieces,
+                [f32(-(-(STEPS + 1) * count // ROWS) * ROWS, slots)],
+                record_scratch + [pltpu.VMEM(record_shape, jnp.float32)],
+                cost=side_cost,
+            )
+        else:
+            state, send = results
+            from_next, from_twin = swap(send, send)
+            records += call(
+                part(record_phase, lay),
+                (),
+                [histories[-1], codes],
+                [f32(*record_shape)],
+                record_scratch,
+                cost=side_cost,
+            )
+
+    misfit_next, misfit_twin = swap(misfit, misfit)
+    state, from_next, from_twin = back_state, back_from_next, back_from_twin
+    gradient = None
+    inject_shape = f32(DEPTH, lay.inner * lay.wide, LANES)
+    for phase in range(phases):
+        first, last = phase == 0, phase == phases - 1
+        (inject,) = call(part(spread_own, lay, phase), (), [misfit], [inject_shape], cost=side_cost)
+        (inject,) = call(
+            part(spread_sides, lay, phase),
+            (where,),
+            [inject, misfit_next, misfit_twin],
+            [inject_shape],
+            cost=side_cost,
+            aliases={1: 0},
+        )
+        results = call(
+            part(backward, lay, phase),
+            (where,),
+            [state, from_next, from_twin, half, gain, inject],
+            [history_shape] + ([] if last else state_shapes),
+            buffers,
+            cost=step_cost,
+        )
+        arrays = [results[0], histories[phases - 1 - phase], states[phases - 1 - phase]]
+        if last:
+            sends = call(
+                part(gradient_last, lay),
+                (where,),
+                arrays + [gradient, misfit],
+                [f32(lay.cells + traces.shape[0], LANES)] * count,
+                [pltpu.VMEM((lay.rows, LANES), jnp.float32)] * 2,
+            )
+            continue
+        _, state, send = results
+        from_next, from_twin = swap(send, send)
+        kernel = gradient_first if first else gradient_later
+        (gradient,) = call(
+            part(kernel, lay), (), arrays + ([] if first else [gradient]), [f32(lay.rows, LANES)], cost=side_cost
+        )
+    pieces = [lax.ppermute(send, axes, lay.to_slabs(turn)) for turn, send in enumerate(sends)]
+    gradient, residual = call(
+        part(finish, lay),
+        (slab_int,),
+        pieces,
+        [f32(lay.width_x * lay.width_y, LANES), f32(*traces.shape)],
+    )
+    return gradient.reshape(courant.shape), residual.reshape(observed.shape)
+
+
+def local(courant, *rest):
+    width_x, width_y, depth_z = courant.shape
+    count_x, count_y = lax.axis_size("gx"), lax.axis_size("gy")
+    if fits(count_x, count_y, width_x, width_y, depth_z):
+        return local_tiles(Layout(count_x, count_y, width_x, width_y), courant, *rest)
+    return local_blocks(courant, *rest)
 
 
 def padded_2(cells, sides, width):
@@ -64,7 +825,7 @@
     return flat.reshape(shape)
 
 
-def local(
+def local_blocks(
     courant,
     state_prev,
     state_now,

time: 539 us -> 142 us (0.26); the launches traced: 532 us -> 141 us
  starting transfers between devices: 197 us -> 61.2 us
  waiting for transfers between devices: 155 us -> 19.2 us
  other arithmetic: 122 us -> 2.91 us
  Pallas kernels: 0 us -> 52.3 us
  local copies, waits for them, and re-layouts: 46.1 us -> 4.63 us
  blocking collectives: 7.99 us -> 0 us
    ppermute x96 -> x26, waiting for transfers between devices: 150 us -> 19.2 us  [the longest x8 14 us: local_tiles(): lax.ppermute(cut, axes, lay.to_chunks(turn))]
    ppermute x96 -> x26, starting transfers between devices: 187 us -> 61.2 us  [the longest x7 28.2 us: swap(): lax.ppermute(to_twin, axes, lay.swaps(0))]
    pallas_call x0 -> x23, Pallas kernels: none -> 52.3 us  [call(): pl.pallas_call(kernel, out_shape=tuple(outs), in_specs=[pl.BlockSpec(memo...]
    scatter-add x24 -> x0, other arithmetic: 49.1 us -> none  [place_sum(): jnp.zeros((shape[0] * shape[1] * shape[2],), jnp.float32).at[indices]]
    gather x12 -> x0, local copies, waits for them, and re-layouts: 37.7 us -> none  [advance(): following.reshape(-1)[cells] * active_flat]
    dynamic_update_slice x12 -> x0, other arithmetic: 29.1 us -> none  [local(): lax.scan(advance, (state_prev, state_now), source_weight)]
    add x12 -> x0, other arithmetic: 21.4 us -> none  [retreat(): return ((current, earlier, gradient + earlier * acceleration), None)]
    select_n x37 -> x2, other arithmetic: 17.2 us -> 0.69 us  [the longest x1 0.68 us: source_rows(): jnp.where(inside, y * lay.stride + (2 * tile + 1) * ROWS + row, ROWS // 2)]
  transfers between devices with their start and end apart: 98 -> 26, of which waited for: 73 -> 5; matrix products, arithmetic and copies ran while one was open for 27% -> 2% of each run, Pallas kernels for 0% -> 20%
where the time goes in v2:
time: 142 us; the launch traced here: 141 us
  starting transfers between devices  61.2 us (43%)
  Pallas kernels  52.3 us (37%)
  waiting for transfers between devices  19.2 us (14%)
  local copies, waits for them, and re-layouts  4.63 us (3%)
  other arithmetic  2.91 us (2%)
    pallas_call x23, Pallas kernels, call(): pl.pallas_call(kernel, out_shape=tuple(outs), in_specs=[pl.BlockSpec(memo...  52.3 us
    ppermute x7, starting transfers between devices, swap(): lax.ppermute(to_twin, axes, lay.swaps(0))  28.2 us
    ppermute x8, starting transfers between devices, local_tiles(): lax.ppermute(cut, axes, lay.to_chunks(turn))  17.8 us
    ppermute x8, waiting for transfers between devices, local_tiles(): lax.ppermute(cut, axes, lay.to_chunks(turn))  14 us
    ppermute x4, starting transfers between devices, local_tiles(): lax.ppermute(send, axes, lay.to_slabs(turn))  9.93 us
    ppermute x7, starting transfers between devices, swap(): lax.ppermute(to_next, axes, lay.swaps(1))  5.2 us
    ppermute x4, waiting for transfers between devices, local_tiles(): lax.ppermute(send, axes, lay.to_slabs(turn))  4.8 us
    unnamed x16, local copies, waits for them, and re-layouts  4.2 us
  transfers between devices with their start and end apart: 26, of which 5 were waited for; matrix products, arithmetic and copies ran while one was open for 2% of the time, Pallas kernels for 20%

profile of v2, /device:TPU:0, one launch (start us, length us, event | category | flops | bytes accessed | tf_op | source)
XLA Modules:
  0.0 141.5 jit_solution(3859477589917548437)
XLA Ops:
  6.8 5.4 %collective-permute-start.7 = (f32[392,128]{1,0:T(8,128)S(1)}, f32[392,128]{1,0:T(8,128)S(1)}, u32[]{:S(2)}, u32[]{:S(2)}) collective-permute-start(f32[392,128]{1,0:T(8,128)S(1)} %get-tuple-element.45), channel_id=1, source_target_pairs={{0,1},{1,9},{2,15},{3,7},{4,0},{5,8},{6,14},{7,6},{8,5},{9,13},{10... | collective-permute-start | bytes 602120 | tf_op jit(solution)/shard_map/ppermute | solution.py:635
  12.2 3.2 %collective-permute-start.9 = (f32[392,128]{1,0:T(8,128)S(1)}, f32[392,128]{1,0:T(8,128)S(1)}, u32[]{:S(2)}, u32[]{:S(2)}) collective-permute-start(f32[392,128]{1,0:T(8,128)S(1)} %get-tuple-element.47), channel_id=1, source_target_pairs={{0,5},{1,13},{2,11},{3,3},{4,4},{5,12},{6,10},{7,2},{8,1},{9,9},{1... | collective-permute-start | bytes 602120 | tf_op jit(solution)/shard_map/ppermute | solution.py:635
  17.4 11.7 %collective-permute-done.8.refs_2_ = f32[392,128]{1,0:T(8,128)S(1)} collective-permute-done((f32[392,128]{1,0:T(8,128)S(1)}, f32[392,128]{1,0:T(8,128)S(1)}, u32[]{:S(2)}, u32[]{:S(2)}) %collective-permute-start.8) | collective-permute-done | bytes 200736 | tf_op jit(solution)/shard_map/ppermute | solution.py:635
  30.6 3.2 %collective-permute-start.11 = (f32[1280,128]{1,0:T(8,128)S(1)}, f32[1280,128]{1,0:T(8,128)S(1)}, u32[]{:S(2)}, u32[]{:S(2)}) collective-permute-start(f32[1280,128]{1,0:T(8,128)S(1)} %get-tuple-element.50), channel_id=1, source_target_pairs={{0,1},{1,0},{4,5},{5,4},{8,9},{9,8},{12,13},{13,12},{14,15},{15,14... | collective-permute-start | bytes 1966088 | tf_op jit(solution)/shard_map/ppermute | solution.py:615
  35.8 5.3 %shard_map.117 = (f32[2048,128]{1,0:T(8,128)S(1)}, f32[1280,128]{1,0:T(8,128)S(1)}, f32[1280,128]{1,0:T(8,128)S(1)}, f32[768,128]{1,0:T(8,128)S(1)}) custom-call(s32[33]{0:T(128)S(1)} %pad_add_fusion.1.ints, f32[1280,128]{1,0:T(8,128)S(1)} %get-tuple-element.48.state, f32[1280,128]{1,0:T(8,128)S(1)} %collective-permute-done.10.from_next, ...), custom_call_target="tpu_custom_call" | custom-call | flops 8000000 | bytes 8000000 | tf_op jit(solution)/shard_map/pallas_call | solution.py:82
  41.8 9.5 %collective-permute-start.13 = (f32[768,128]{1,0:T(8,128)S(1)}, f32[768,128]{1,0:T(8,128)S(1)}, u32[]{:S(2)}, u32[]{:S(2)}) collective-permute-start(f32[768,128]{1,0:T(8,128)S(1)} %get-tuple-element.54), channel_id=1, source_target_pairs={{0,1},{1,0},{4,5},{5,4},{8,9},{9,8},{12,13},{13,12},{14,15},{15,14... | collective-permute-start | bytes 1179656 | tf_op jit(solution)/shard_map/ppermute | solution.py:615
  52.2 3.6 %collective-permute-start.1 = (f32[304,128]{1,0:T(8,128)S(1)}, f32[304,128]{1,0:T(8,128)S(1)}, u32[]{:S(2)}, u32[]{:S(2)}) collective-permute-start(f32[304,128]{1,0:T(8,128)S(1)} %get-tuple-element.38), channel_id=1, source_target_pairs={{0,1},{1,9},{2,15},{3,7},{4,0},{5,8},{6,14},{7,6},{8,5},{9,13},{10... | collective-permute-start | bytes 466952 | tf_op jit(solution)/shard_map/ppermute | solution.py:655
  55.8 4.1 %collective-permute-start.3 = (f32[304,128]{1,0:T(8,128)S(1)}, f32[304,128]{1,0:T(8,128)S(1)}, u32[]{:S(2)}, u32[]{:S(2)}) collective-permute-start(f32[304,128]{1,0:T(8,128)S(1)} %get-tuple-element.40), channel_id=1, source_target_pairs={{0,5},{1,13},{2,11},{3,3},{4,4},{5,12},{6,10},{7,2},{8,1},{9,9},{1... | collective-permute-start | bytes 466952 | tf_op jit(solution)/shard_map/ppermute | solution.py:655
  60.0 5.2 %shard_map.118 = (f32[2048,128]{1,0:T(8,128)S(1)}, f32[1280,128]{1,0:T(8,128)S(1)}, f32[768,128]{1,0:T(8,128)S(1)}) custom-call(s32[33]{0:T(128)S(1)} %pad_add_fusion.1.ints, f32[1280,128]{1,0:T(8,128)S(1)} %get-tuple-element.53.state, f32[768,128]{1,0:T(8,128)S(1)} %collective-permute-done.12.from_next, f32[768,128]{1,0:T(8,128)S(1)} %collective-permute-done.13.from_twin, ...), custom_call_target="tpu_custom_call" | custom-call | flops 8000000 | bytes 8000000 | tf_op jit(solution)/shard_map/pallas_call | solution.py:82
  67.5 2.3 %collective-permute-done.2.refs_2_.refs_4_ = f32[304,128]{1,0:T(8,128)S(1)} collective-permute-done((f32[304,128]{1,0:T(8,128)S(1)}, f32[304,128]{1,0:T(8,128)S(1)}, u32[]{:S(2)}, u32[]{:S(2)}) %collective-permute-start.2) | collective-permute-done | bytes 155680 | tf_op jit(solution)/shard_map/ppermute | solution.py:655
  71.2 2.9 %collective-permute-start.5 = (f32[896,128]{1,0:T(8,128)S(1)}, f32[896,128]{1,0:T(8,128)S(1)}, u32[]{:S(2)}, u32[]{:S(2)}) collective-permute-start(f32[896,128]{1,0:T(8,128)S(1)} %get-tuple-element.43), channel_id=1, source_target_pairs={{0,1},{1,0},{4,5},{5,4},{8,9},{9,8},{12,13},{13,12},{14,15},{15,14... | collective-permute-start | bytes 1376264 | tf_op jit(solution)/shard_map/ppermute | solution.py:615
  76.9 5.2 %shard_map.119.history = f32[2048,128]{1,0:T(8,128)S(1)} custom-call(s32[33]{0:T(128)S(1)} %pad_add_fusion.1.ints, f32[1280,128]{1,0:T(8,128)S(1)} %get-tuple-element.55.state, f32[768,128]{1,0:T(8,128)S(1)} %collective-permute-done.14.from_next, f32[768,128]{1,0:T(8,128)S(1)} %collective-permute-done.15.from_twin, ...), custom_call_target="tpu_custom_call" | custom-call | flops 8000000 | bytes 8000000 | tf_op jit(solution)/shard_map/pallas_call | solution.py:82
  84.9 3.1 %collective-permute-start.17 = (f32[56,512]{1,0:T(8,128)S(1)}, f32[56,512]{1,0:T(8,128)S(1)}, u32[]{:S(2)}, u32[]{:S(2)}) collective-permute-start(f32[56,512]{1,0:T(8,128)S(1)} %shard_map.122.misfit), channel_id=1, source_target_pairs={{0,1},{1,0},{4,5},{5,4},{8,9},{9,8},{12,13},{13,12},{14,15},{15,14... | collective-permute-start | bytes 344072 | tf_op jit(solution)/shard_map/ppermute | solution.py:615
  89.8 2.0 %shard_map.124.inject = f32[4,1280,128]{2,1,0:T(8,128)S(1)} custom-call(s32[2]{0:T(128)S(1)} %pad_add_fusion.where_ref, f32[4,1280,128]{2,1,0:T(8,128)S(1)} %shard_map.123.own, f32[56,512]{1,0:T(8,128)S(1)} %collective-permute-done.16.misfit_next, f32[56,512]{1,0:T(8,128)S(1)} %collective-permute-done.17.misfit_twin), custom_call_target="tpu_custom_call", output_to_operand_aliasing={{}: (1, {})} | custom-call | flops 4000000 | bytes 4000000 | tf_op jit(solution)/shard_map/pallas_call | solution.py:82
  91.8 5.2 %shard_map.125 = (f32[2048,128]{1,0:T(8,128)S(1)}, f32[1280,128]{1,0:T(8,128)S(1)}, f32[768,128]{1,0:T(8,128)S(1)}) custom-call(s32[2]{0:T(128)S(1)} %pad_add_fusion.where_ref, f32[1280,128]{1,0:T(8,128)S(1)} %get-tuple-element.41.state, f32[896,128]{1,0:T(8,128)S(1)} %collective-permute-done.4.from_next, f32[896,128]{1,0:T(8,128)S(1)} %collective-permute-done.5.from_twin, ...), custom_call_target="tpu_custom_call" | custom-call | flops 8000000 | bytes 8000000 | tf_op jit(solution)/shard_map/pallas_call | solution.py:82
  97.7 3.4 %collective-permute-start.19 = (f32[768,128]{1,0:T(8,128)S(1)}, f32[768,128]{1,0:T(8,128)S(1)}, u32[]{:S(2)}, u32[]{:S(2)}) collective-permute-start(f32[768,128]{1,0:T(8,128)S(1)} %get-tuple-element.61), channel_id=1, source_target_pairs={{0,1},{1,0},{4,5},{5,4},{8,9},{9,8},{12,13},{13,12},{14,15},{15,14... | collective-permute-start | bytes 1179656 | tf_op jit(solution)/shard_map/ppermute | solution.py:615
  102.9 2.0 %shard_map.127.inject = f32[4,1280,128]{2,1,0:T(8,128)S(1)} custom-call(s32[2]{0:T(128)S(1)} %pad_add_fusion.where_ref, f32[4,1280,128]{2,1,0:T(8,128)S(1)} %shard_map.126.own, f32[56,512]{1,0:T(8,128)S(1)} %collective-permute-done.16.misfit_next, f32[56,512]{1,0:T(8,128)S(1)} %collective-permute-done.17.misfit_twin), custom_call_target="tpu_custom_call", output_to_operand_aliasing={{}: (1, {})} | custom-call | flops 4000000 | bytes 4000000 | tf_op jit(solution)/shard_map/pallas_call | solution.py:82
  105.0 5.2 %shard_map.128 = (f32[2048,128]{1,0:T(8,128)S(1)}, f32[1280,128]{1,0:T(8,128)S(1)}, f32[768,128]{1,0:T(8,128)S(1)}) custom-call(s32[2]{0:T(128)S(1)} %pad_add_fusion.where_ref, f32[1280,128]{1,0:T(8,128)S(1)} %get-tuple-element.60.state, f32[768,128]{1,0:T(8,128)S(1)} %collective-permute-done.18.from_next, f32[768,128]{1,0:T(8,128)S(1)} %collective-permute-done.19.from_twin, ...), custom_call_target="tpu_custom_call" | custom-call | flops 8000000 | bytes 8000000 | tf_op jit(solution)/shard_map/pallas_call | solution.py:82
  111.0 4.5 %collective-permute-start.21 = (f32[768,128]{1,0:T(8,128)S(1)}, f32[768,128]{1,0:T(8,128)S(1)}, u32[]{:S(2)}, u32[]{:S(2)}) collective-permute-start(f32[768,128]{1,0:T(8,128)S(1)} %get-tuple-element.63), channel_id=1, source_target_pairs={{0,1},{1,0},{4,5},{5,4},{8,9},{9,8},{12,13},{13,12},{14,15},{15,14... | collective-permute-start | bytes 1179656 | tf_op jit(solution)/shard_map/ppermute | solution.py:615
  117.7 2.0 %shard_map.130.inject = f32[4,1280,128]{2,1,0:T(8,128)S(1)} custom-call(s32[2]{0:T(128)S(1)} %pad_add_fusion.where_ref, f32[4,1280,128]{2,1,0:T(8,128)S(1)} %shard_map.129.own, f32[56,512]{1,0:T(8,128)S(1)} %collective-permute-done.16.misfit_next, f32[56,512]{1,0:T(8,128)S(1)} %collective-permute-done.17.misfit_twin), custom_call_target="tpu_custom_call", output_to_operand_aliasing={{}: (1, {})} | custom-call | flops 4000000 | bytes 4000000 | tf_op jit(solution)/shard_map/pallas_call | solution.py:82
  120.0 5.1 %shard_map.131.adjoint = f32[2048,128]{1,0:T(8,128)S(1)} custom-call(s32[2]{0:T(128)S(1)} %pad_add_fusion.where_ref, f32[1280,128]{1,0:T(8,128)S(1)} %get-tuple-element.62.state, f32[768,128]{1,0:T(8,128)S(1)} %collective-permute-done.20.from_next, f32[768,128]{1,0:T(8,128)S(1)} %collective-permute-done.21.from_twin, ...), custom_call_target="tpu_custom_call" | custom-call | flops 8000000 | bytes 8000000 | tf_op jit(solution)/shard_map/pallas_call | solution.py:82
  126.6 4.5 %collective-permute-start.23 = (f32[176,128]{1,0:T(8,128)S(1)}, f32[176,128]{1,0:T(8,128)S(1)}, u32[]{:S(2)}, u32[]{:S(2)}) collective-permute-start(f32[176,128]{1,0:T(8,128)S(1)} %get-tuple-element.67), channel_id=1, source_target_pairs={{1,0},{9,1},{15,2},{7,3},{0,4},{8,5},{14,6},{6,7},{5,8},{13,9},{11... | collective-permute-start | bytes 270344 | tf_op jit(solution)/shard_map/ppermute | solution.py:757
  131.1 2.9 %collective-permute-start.24 = (f32[176,128]{1,0:T(8,128)S(1)}, f32[176,128]{1,0:T(8,128)S(1)}, u32[]{:S(2)}, u32[]{:S(2)}) collective-permute-start(f32[176,128]{1,0:T(8,128)S(1)} %get-tuple-element.68), channel_id=1, source_target_pairs={{4,0},{12,1},{10,2},{2,3},{5,4},{13,5},{11,6},{3,7},{0,8},{8,9},{1... | collective-permute-start | bytes 270344 | tf_op jit(solution)/shard_map/ppermute | solution.py:757
  137.5 3.2 %collective-permute-done.25.refs_3_ = f32[176,128]{1,0:T(8,128)S(1)} collective-permute-done((f32[176,128]{1,0:T(8,128)S(1)}, f32[176,128]{1,0:T(8,128)S(1)}, u32[]{:S(2)}, u32[]{:S(2)}) %collective-permute-start.25) | collective-permute-done | bytes 90144 | tf_op jit(solution)/shard_map/ppermute | solution.py:757
  (83 shorter events, 35.7 us)
Async XLA Ops:
  6.0 11.4 %collective-permute-start.6 = (f32[392,128]{1,0:T(8,128)S(1)}, f32[392,128]{1,0:T(8,128)S(1)}, u32[]{:S(2)}, u32[]{:S(2)}) collective-permute-start(f32[392,128]{1,0:T(8,128)S(1)} %get-tuple-element.44), channel_id=1, source_target_pairs={{0,0},{1,8},{2,14},{3,6},{4,1},{5,9},{6,15},{7,7},{8,4},{9,12},{10... | collective-permute-start | bytes 602120 | tf_op jit(solution)/shard_map/ppermute | solution.py:635
  6.8 10.6 %collective-permute-start.7 = (f32[392,128]{1,0:T(8,128)S(1)}, f32[392,128]{1,0:T(8,128)S(1)}, u32[]{:S(2)}, u32[]{:S(2)}) collective-permute-start(f32[392,128]{1,0:T(8,128)S(1)} %get-tuple-element.45), channel_id=1, source_target_pairs={{0,1},{1,9},{2,15},{3,7},{4,0},{5,8},{6,14},{7,6},{8,5},{9,13},{10... | collective-permute-start | bytes 602120 | tf_op jit(solution)/shard_map/ppermute | solution.py:635
  12.2 16.8 %collective-permute-start.8 = (f32[392,128]{1,0:T(8,128)S(1)}, f32[392,128]{1,0:T(8,128)S(1)}, u32[]{:S(2)}, u32[]{:S(2)}) collective-permute-start(f32[392,128]{1,0:T(8,128)S(1)} %get-tuple-element.46), channel_id=1, source_target_pairs={{0,4},{1,12},{2,10},{3,2},{4,5},{5,13},{6,11},{7,3},{8,0},{9,8},{1... | collective-permute-start | bytes 602120 | tf_op jit(solution)/shard_map/ppermute | solution.py:635
  12.2 16.8 %collective-permute-start.9 = (f32[392,128]{1,0:T(8,128)S(1)}, f32[392,128]{1,0:T(8,128)S(1)}, u32[]{:S(2)}, u32[]{:S(2)}) collective-permute-start(f32[392,128]{1,0:T(8,128)S(1)} %get-tuple-element.47), channel_id=1, source_target_pairs={{0,5},{1,13},{2,11},{3,3},{4,4},{5,12},{6,10},{7,2},{8,1},{9,9},{1... | collective-permute-start | bytes 602120 | tf_op jit(solution)/shard_map/ppermute | solution.py:635
  29.9 5.3 %collective-permute-start.10 = (f32[1280,128]{1,0:T(8,128)S(1)}, f32[1280,128]{1,0:T(8,128)S(1)}, u32[]{:S(2)}, u32[]{:S(2)}) collective-permute-start(f32[1280,128]{1,0:T(8,128)S(1)} %get-tuple-element.49), channel_id=1, source_target_pairs={{1,4},{4,1},{5,8},{8,5},{9,12},{12,9},{13,14},{14,13},{15,10},{10,... | collective-permute-start | bytes 1966088 | tf_op jit(solution)/shard_map/ppermute | solution.py:614
  41.1 14.8 %collective-permute-start.12 = (f32[768,128]{1,0:T(8,128)S(1)}, f32[768,128]{1,0:T(8,128)S(1)}, u32[]{:S(2)}, u32[]{:S(2)}) collective-permute-start(f32[768,128]{1,0:T(8,128)S(1)} %get-tuple-element.54), channel_id=1, source_target_pairs={{1,4},{4,1},{5,8},{8,5},{9,12},{12,9},{13,14},{14,13},{15,10},{10,... | collective-permute-start | bytes 1179656 | tf_op jit(solution)/shard_map/ppermute | solution.py:614
  41.8 18.2 %collective-permute-start.13 = (f32[768,128]{1,0:T(8,128)S(1)}, f32[768,128]{1,0:T(8,128)S(1)}, u32[]{:S(2)}, u32[]{:S(2)}) collective-permute-start(f32[768,128]{1,0:T(8,128)S(1)} %get-tuple-element.54), channel_id=1, source_target_pairs={{0,1},{1,0},{4,5},{5,4},{8,9},{9,8},{12,13},{13,12},{14,15},{15,14... | collective-permute-start | bytes 1179656 | tf_op jit(solution)/shard_map/ppermute | solution.py:615
  51.6 14.3 %collective-permute-start = (f32[304,128]{1,0:T(8,128)S(1)}, f32[304,128]{1,0:T(8,128)S(1)}, u32[]{:S(2)}, u32[]{:S(2)}) collective-permute-start(f32[304,128]{1,0:T(8,128)S(1)} %get-tuple-element.37), channel_id=1, source_target_pairs={{0,0},{1,8},{2,14},{3,6},{4,1},{5,9},{6,15},{7,7},{8,4},{9,12},{10... | collective-permute-start | bytes 466952 | tf_op jit(solution)/shard_map/ppermute | solution.py:655
  52.2 15.3 %collective-permute-start.1 = (f32[304,128]{1,0:T(8,128)S(1)}, f32[304,128]{1,0:T(8,128)S(1)}, u32[]{:S(2)}, u32[]{:S(2)}) collective-permute-start(f32[304,128]{1,0:T(8,128)S(1)} %get-tuple-element.38), channel_id=1, source_target_pairs={{0,1},{1,9},{2,15},{3,7},{4,0},{5,8},{6,14},{7,6},{8,5},{9,13},{10... | collective-permute-start | bytes 466952 | tf_op jit(solution)/shard_map/ppermute | solution.py:655
  55.8 14.0 %collective-permute-start.2 = (f32[304,128]{1,0:T(8,128)S(1)}, f32[304,128]{1,0:T(8,128)S(1)}, u32[]{:S(2)}, u32[]{:S(2)}) collective-permute-start(f32[304,128]{1,0:T(8,128)S(1)} %get-tuple-element.39), channel_id=1, source_target_pairs={{0,4},{1,12},{2,10},{3,2},{4,5},{5,13},{6,11},{7,3},{8,0},{9,8},{1... | collective-permute-start | bytes 466952 | tf_op jit(solution)/shard_map/ppermute | solution.py:655
  55.8 13.9 %collective-permute-start.3 = (f32[304,128]{1,0:T(8,128)S(1)}, f32[304,128]{1,0:T(8,128)S(1)}, u32[]{:S(2)}, u32[]{:S(2)}) collective-permute-start(f32[304,128]{1,0:T(8,128)S(1)} %get-tuple-element.40), channel_id=1, source_target_pairs={{0,5},{1,13},{2,11},{3,3},{4,4},{5,12},{6,10},{7,2},{8,1},{9,9},{1... | collective-permute-start | bytes 466952 | tf_op jit(solution)/shard_map/ppermute | solution.py:655
  65.2 11.7 %collective-permute-start.14 = (f32[768,128]{1,0:T(8,128)S(1)}, f32[768,128]{1,0:T(8,128)S(1)}, u32[]{:S(2)}, u32[]{:S(2)}) collective-permute-start(f32[768,128]{1,0:T(8,128)S(1)} %get-tuple-element.56), channel_id=1, source_target_pairs={{1,4},{4,1},{5,8},{8,5},{9,12},{12,9},{13,14},{14,13},{15,10},{10,... | collective-permute-start | bytes 1179656 | tf_op jit(solution)/shard_map/ppermute | solution.py:614
  65.9 11.0 %collective-permute-start.15 = (f32[768,128]{1,0:T(8,128)S(1)}, f32[768,128]{1,0:T(8,128)S(1)}, u32[]{:S(2)}, u32[]{:S(2)}) collective-permute-start(f32[768,128]{1,0:T(8,128)S(1)} %get-tuple-element.56), channel_id=1, source_target_pairs={{0,1},{1,0},{4,5},{5,4},{8,9},{9,8},{12,13},{13,12},{14,15},{15,14... | collective-permute-start | bytes 1179656 | tf_op jit(solution)/shard_map/ppermute | solution.py:615
  70.5 21.3 %collective-permute-start.4 = (f32[896,128]{1,0:T(8,128)S(1)}, f32[896,128]{1,0:T(8,128)S(1)}, u32[]{:S(2)}, u32[]{:S(2)}) collective-permute-start(f32[896,128]{1,0:T(8,128)S(1)} %get-tuple-element.42), channel_id=1, source_target_pairs={{1,4},{4,1},{5,8},{8,5},{9,12},{12,9},{13,14},{14,13},{15,10},{10,... | collective-permute-start | bytes 1376264 | tf_op jit(solution)/shard_map/ppermute | solution.py:614
  71.2 20.6 %collective-permute-start.5 = (f32[896,128]{1,0:T(8,128)S(1)}, f32[896,128]{1,0:T(8,128)S(1)}, u32[]{:S(2)}, u32[]{:S(2)}) collective-permute-start(f32[896,128]{1,0:T(8,128)S(1)} %get-tuple-element.43), channel_id=1, source_target_pairs={{0,1},{1,0},{4,5},{5,4},{8,9},{9,8},{12,13},{13,12},{14,15},{15,14... | collective-permute-start | bytes 1376264 | tf_op jit(solution)/shard_map/ppermute | solution.py:615
  84.0 5.7 %collective-permute-start.16 = (f32[56,512]{1,0:T(8,128)S(1)}, f32[56,512]{1,0:T(8,128)S(1)}, u32[]{:S(2)}, u32[]{:S(2)}) collective-permute-start(f32[56,512]{1,0:T(8,128)S(1)} %shard_map.122.misfit), channel_id=1, source_target_pairs={{1,4},{4,1},{5,8},{8,5},{9,12},{12,9},{13,14},{14,13},{15,10},{10,... | collective-permute-start | bytes 344072 | tf_op jit(solution)/shard_map/ppermute | solution.py:614
  97.0 7.9 %collective-permute-start.18 = (f32[768,128]{1,0:T(8,128)S(1)}, f32[768,128]{1,0:T(8,128)S(1)}, u32[]{:S(2)}, u32[]{:S(2)}) collective-permute-start(f32[768,128]{1,0:T(8,128)S(1)} %get-tuple-element.61), channel_id=1, source_target_pairs={{1,4},{4,1},{5,8},{8,5},{9,12},{12,9},{13,14},{14,13},{15,10},{10,... | collective-permute-start | bytes 1179656 | tf_op jit(solution)/shard_map/ppermute | solution.py:614
  97.7 7.2 %collective-permute-start.19 = (f32[768,128]{1,0:T(8,128)S(1)}, f32[768,128]{1,0:T(8,128)S(1)}, u32[]{:S(2)}, u32[]{:S(2)}) collective-permute-start(f32[768,128]{1,0:T(8,128)S(1)} %get-tuple-element.61), channel_id=1, source_target_pairs={{0,1},{1,0},{4,5},{5,4},{8,9},{9,8},{12,13},{13,12},{14,15},{15,14... | collective-permute-start | bytes 1179656 | tf_op jit(solution)/shard_map/ppermute | solution.py:615
  110.1 9.8 %collective-permute-start.20 = (f32[768,128]{1,0:T(8,128)S(1)}, f32[768,128]{1,0:T(8,128)S(1)}, u32[]{:S(2)}, u32[]{:S(2)}) collective-permute-start(f32[768,128]{1,0:T(8,128)S(1)} %get-tuple-element.63), channel_id=1, source_target_pairs={{1,4},{4,1},{5,8},{8,5},{9,12},{12,9},{13,14},{14,13},{15,10},{10,... | collective-permute-start | bytes 1179656 | tf_op jit(solution)/shard_map/ppermute | solution.py:614
  111.0 8.9 %collective-permute-start.21 = (f32[768,128]{1,0:T(8,128)S(1)}, f32[768,128]{1,0:T(8,128)S(1)}, u32[]{:S(2)}, u32[]{:S(2)}) collective-permute-start(f32[768,128]{1,0:T(8,128)S(1)} %get-tuple-element.63), channel_id=1, source_target_pairs={{0,1},{1,0},{4,5},{5,4},{8,9},{9,8},{12,13},{13,12},{14,15},{15,14... | collective-permute-start | bytes 1179656 | tf_op jit(solution)/shard_map/ppermute | solution.py:615
  125.9 10.0 %collective-permute-start.22 = (f32[176,128]{1,0:T(8,128)S(1)}, f32[176,128]{1,0:T(8,128)S(1)}, u32[]{:S(2)}, u32[]{:S(2)}) collective-permute-start(f32[176,128]{1,0:T(8,128)S(1)} %get-tuple-element.66), channel_id=1, source_target_pairs={{0,0},{8,1},{14,2},{6,3},{1,4},{9,5},{15,6},{7,7},{4,8},{12,9},{10... | collective-permute-start | bytes 270344 | tf_op jit(solution)/shard_map/ppermute | solution.py:757
  126.6 9.3 %collective-permute-start.23 = (f32[176,128]{1,0:T(8,128)S(1)}, f32[176,128]{1,0:T(8,128)S(1)}, u32[]{:S(2)}, u32[]{:S(2)}) collective-permute-start(f32[176,128]{1,0:T(8,128)S(1)} %get-tuple-element.67), channel_id=1, source_target_pairs={{1,0},{9,1},{15,2},{7,3},{0,4},{8,5},{14,6},{6,7},{5,8},{13,9},{11... | collective-permute-start | bytes 270344 | tf_op jit(solution)/shard_map/ppermute | solution.py:757
  131.1 6.4 %collective-permute-start.24 = (f32[176,128]{1,0:T(8,128)S(1)}, f32[176,128]{1,0:T(8,128)S(1)}, u32[]{:S(2)}, u32[]{:S(2)}) collective-permute-start(f32[176,128]{1,0:T(8,128)S(1)} %get-tuple-element.68), channel_id=1, source_target_pairs={{4,0},{12,1},{10,2},{2,3},{5,4},{13,5},{11,6},{3,7},{0,8},{8,9},{1... | collective-permute-start | bytes 270344 | tf_op jit(solution)/shard_map/ppermute | solution.py:757
  134.0 6.7 %collective-permute-start.25 = (f32[176,128]{1,0:T(8,128)S(1)}, f32[176,128]{1,0:T(8,128)S(1)}, u32[]{:S(2)}, u32[]{:S(2)}) collective-permute-start(f32[176,128]{1,0:T(8,128)S(1)} %get-tuple-element.69), channel_id=1, source_target_pairs={{5,0},{13,1},{11,2},{3,3},{4,4},{12,5},{10,6},{2,7},{1,8},{9,9},{1... | collective-permute-start | bytes 270344 | tf_op jit(solution)/shard_map/ppermute | solution.py:757
  (10 other events, 149.9 us)
